TPU v7x, 128 devices: a whole 4x4x4 slice. The times are simulated.
128 devices in a mesh: exp: 32 (over z, x, core), hid: 4 (over y).
Axes of the slice: x: 4, y: 4, z: 4, core: 2. Of those that a mesh axis runs over, the one named last changes fastest.
Arguments:
- block_input: bfloat16 [32768, 1024], P(('exp', 'hid')), may hold values from -6 to 6
- norm1_gain: float32 [1024], replicated, may hold values from 0.1 to 1.9
- norm1_bias: float32 [1024], replicated, may hold values from -1.5 to 1.5
- w_qkv: bfloat16 [3, 1024, 1024], P(None, None, 'hid'), may hold values from -0.1875 to 0.1875
- w_out: bfloat16 [1024, 1024], P('hid'), may hold values from -1 to 1
- norm2_gain: float32 [1024], replicated, may hold values from 0.1 to 1.9
- norm2_bias: float32 [1024], replicated, may hold values from -1.5 to 1.5
- w_in: bfloat16 [64, 1024, 4096], P('exp', None, 'hid'), may hold values from -0.1875 to 0.1875
- w_down: bfloat16 [64, 4096, 1024], P('exp', 'hid'), may hold values from -0.09375 to 0.09375
- expert_ids: int32 [32768, 1], P(('exp', 'hid')), may hold values from 0 to 63; in each aligned block of 256 rows (0 to 255, 256 to 511, ...) at most 8 rows name the same one
- out_grad: bfloat16 [32768, 1024], P(('exp', 'hid')), may hold values from -6 to 6
Outputs:
- output: bfloat16 [32768, 1024], P(('exp', 'hid'))
- grad_input: float32 [32768, 1024], P(('exp', 'hid'))
- d_norm1_gain: float32 [1024], replicated
- d_norm1_bias: float32 [1024], replicated
- d_w_qkv: float32 [3, 1024, 1024], P(None, None, 'hid')
- d_w_out: float32 [1024, 1024], P('hid')
- d_norm2_gain: float32 [1024], replicated
- d_norm2_bias: float32 [1024], replicated
- d_w_in: float32 [64, 1024, 4096], P('exp', None, 'hid')
- d_w_down: float32 [64, 4096, 1024], P('exp', 'hid')
Inputs may be any that keep to these rules, and one draw needn't show every extreme that they name: `expert_ids`: among the 256 rows of one device, at most 8 name the same expert, and in every draw some expert is named by exactly 8 rows of some device.
All inputs are finite; a program needn't handle non-finite values.
Results may differ from a plain program's by a relative error of at most 0.02.
Values may be sent and summed in bfloat16 or wider, within the bound.
A program may use at most 192 MiB of HBM per device.

v0:
```python
import jax
import jax.numpy as jnp
from jax import lax
from jax.sharding import PartitionSpec as P

HD = 64
SEQ_MAX = 1024


EPSILON = 1e-05
NEG_LARGE = -1e30


def layer_norm(vectors, norm_gain, norm_bias):
    row_mean = jnp.mean(vectors, -1, keepdims=True)
    centered = vectors - row_mean
    variance = jnp.mean(centered * centered, -1, keepdims=True)
    return centered * lax.rsqrt(variance + EPSILON) * norm_gain + norm_bias


def smooth_act(pre_act):
    return jax.nn.gelu(pre_act, approximate=True)


def join_rows(token_rows):
    return lax.all_gather(token_rows, "hid", axis=0, tiled=True)


def spread_rows(term_of, own_rows):
    return lax.psum_scatter(
        term_of(jnp.int32(0), own_rows * lax.axis_size("hid")).astype(jnp.bfloat16),
        "hid",
        scatter_dimension=0,
        tiled=True,
    ).astype(jnp.float32)


def to_experts(buffer):
    arrived = lax.all_to_all(buffer, "exp", split_axis=0, concat_axis=0, tiled=True)
    return lax.all_gather(arrived, "hid", axis=0, tiled=True)


def from_experts(term_of, total_rows):
    hid_size = lax.axis_size("hid")
    summed = lax.psum_scatter(
        term_of(jnp.int32(0), total_rows // hid_size * lax.axis_size("hid")).astype(jnp.bfloat16),
        "hid",
        scatter_dimension=0,
        tiled=True,
    )
    return lax.all_to_all(summed, "exp", split_axis=0, concat_axis=0, tiled=True)


def causal_grid(first_row, row_count, key_count):
    query_pos = first_row + jnp.arange(row_count, dtype=jnp.int32)
    return jnp.arange(key_count, dtype=jnp.int32)[None, :] <= query_pos[:, None]


def attend_block(query_block, key_seq, value_seq, first_row, score_scale):
    scores = (
        jnp.einsum("qhd,khd->hqk", query_block, key_seq, preferred_element_type=jnp.float32)
        * score_scale
    )
    allowed = causal_grid(first_row, query_block.shape[0], key_seq.shape[0])
    scores = jnp.where(allowed[None], scores, NEG_LARGE)
    row_max = jnp.max(scores, -1, keepdims=True)
    exp_scores = jnp.exp(scores - row_max)
    exp_total = jnp.sum(exp_scores, -1, keepdims=True)
    attn_probs = (exp_scores / exp_total).astype(jnp.bfloat16)
    heads_out = jnp.einsum(
        "hqk,khd->qhd", attn_probs, value_seq, preferred_element_type=jnp.float32
    )
    return (heads_out.astype(jnp.bfloat16), row_max[..., 0] + jnp.log(exp_total[..., 0]))


def attend_back(query_block, key_seq, value_seq, grad_block, log_total, first_row, score_scale):
    scores = (
        jnp.einsum("qhd,khd->hqk", query_block, key_seq, preferred_element_type=jnp.float32)
        * score_scale
    )
    allowed = causal_grid(first_row, query_block.shape[0], key_seq.shape[0])
    attn_probs = jnp.where(allowed[None], jnp.exp(scores - log_total[:, :, None]), 0.0)
    probs_low = attn_probs.astype(jnp.bfloat16)
    grad_probs = jnp.einsum(
        "qhd,khd->hqk", grad_block, value_seq, preferred_element_type=jnp.float32
    )
    row_inner = jnp.sum(attn_probs * grad_probs, -1, keepdims=True)
    grad_scores = (attn_probs * (grad_probs - row_inner)).astype(jnp.bfloat16)
    grad_query = (
        jnp.einsum("hqk,khd->qhd", grad_scores, key_seq, preferred_element_type=jnp.float32)
        * score_scale
    )
    grad_key = (
        jnp.einsum("hqk,qhd->khd", grad_scores, query_block, preferred_element_type=jnp.float32)
        * score_scale
    )
    grad_value = jnp.einsum(
        "hqk,qhd->khd", probs_low, grad_block, preferred_element_type=jnp.float32
    )
    return (grad_query, grad_key, grad_value)


def on_device(
    block_input,
    norm1_gain,
    norm1_bias,
    w_qkv,
    w_out,
    norm2_gain,
    norm2_bias,
    w_in,
    w_down,
    expert_ids,
    out_grad,
):
    tok_rows, model_width = block_input.shape
    hid_size = lax.axis_size("hid")
    exp_size = lax.axis_size("exp")
    group_rows = tok_rows * hid_size
    length = min(SEQ_MAX, group_rows)
    block_rows = min(512, length)
    seq_count = group_rows // length
    blocks = length // block_rows
    pair_count = seq_count * blocks
    heads_here = w_qkv.shape[2] // HD
    score_scale = HD ** (-0.5)
    inputs32 = block_input.astype(jnp.float32)
    normed, norm1_back = jax.vjp(layer_norm, inputs32, norm1_gain, norm1_bias)
    joined = join_rows(normed.astype(jnp.bfloat16))
    projected = jnp.einsum("td,idh->ith", joined, w_qkv, preferred_element_type=jnp.float32).astype(
        jnp.bfloat16
    )
    stacked = projected.reshape(3, seq_count, length, heads_here, HD)
    queries, keys_all, values_all = (stacked[0], stacked[1], stacked[2])

    def pair_inputs(pair_index):
        seq_index = pair_index // blocks
        first_row = pair_index % blocks * block_rows
        query_seq = lax.dynamic_index_in_dim(queries, seq_index, 0, keepdims=False)
        query_block = lax.dynamic_slice_in_dim(query_seq, first_row, block_rows, 0)
        key_seq = lax.dynamic_index_in_dim(keys_all, seq_index, 0, keepdims=False)
        value_seq = lax.dynamic_index_in_dim(values_all, seq_index, 0, keepdims=False)
        return (query_block, key_seq, value_seq, first_row)

    def forward_pair(pair_index):
        query_block, key_seq, value_seq, first_row = pair_inputs(pair_index)
        return attend_block(query_block, key_seq, value_seq, first_row, score_scale)

    attn_blocks, log_totals = lax.map(forward_pair, jnp.arange(pair_count, dtype=jnp.int32))
    attn_out = attn_blocks.reshape(group_rows, heads_here * HD)

    def attn_term(first_row, row_count):
        return jnp.dot(attn_out, w_out, preferred_element_type=jnp.float32)

    attn_sum = spread_rows(attn_term, tok_rows)
    residual = inputs32 + attn_sum
    normed_two, norm2_back = jax.vjp(layer_norm, residual, norm2_gain, norm2_bias)
    routed = normed_two.astype(jnp.bfloat16)
    experts_here = w_in.shape[0]
    experts_all = experts_here * exp_size
    capacity = 2 * tok_rows // experts_all
    slot_rows = experts_here * capacity
    picked = expert_ids[:, 0]
    one_hot = (picked[:, None] == jnp.arange(experts_all, dtype=jnp.int32)[None, :]).astype(
        jnp.int32
    )
    running = jnp.cumsum(one_hot, 0)
    position = jnp.sum(running * one_hot, 1) - 1
    slot_of = picked * capacity + position
    slot_token = jnp.full((experts_all * capacity,), tok_rows, jnp.int32)
    slot_token = slot_token.at[slot_of].set(jnp.arange(tok_rows, dtype=jnp.int32))
    send_rows = jnp.take(routed, slot_token, axis=0, mode="fill", fill_value=0)
    grad_send = jnp.take(out_grad, slot_token, axis=0, mode="fill", fill_value=0)
    arrived = to_experts(send_rows)
    sources = arrived.shape[0] // slot_rows
    gathered = arrived.reshape(sources, experts_here, capacity, model_width)
    hidden_pre = jnp.einsum("slcd,ldf->slcf", gathered, w_in, preferred_element_type=jnp.float32)
    activated = smooth_act(hidden_pre).astype(jnp.bfloat16)

    def down_term(first_row, row_count):
        partial_value = jnp.einsum(
            "slcf,lfd->slcd", activated, w_down, preferred_element_type=jnp.float32
        )
        return partial_value.reshape(row_count, model_width)

    mixed_slots = from_experts(down_term, sources * slot_rows)
    mixed_rows = jnp.take(mixed_slots, slot_of, axis=0).astype(jnp.float32)
    output = (residual + mixed_rows).astype(jnp.bfloat16)
    grad_out = out_grad.astype(jnp.float32)
    grad_arrived = to_experts(grad_send)
    grad_rows = grad_arrived.reshape(sources, experts_here, capacity, model_width)
    grad_act = jnp.einsum("slcd,lfd->slcf", grad_rows, w_down, preferred_element_type=jnp.float32)
    grad_pre = jax.vjp(smooth_act, hidden_pre)[1](grad_act)[0].astype(jnp.bfloat16)
    d_w_down = jnp.einsum(
        "slcf,slcd->lfd", activated, grad_rows, preferred_element_type=jnp.float32
    )
    d_w_in = jnp.einsum("slcd,slcf->ldf", gathered, grad_pre, preferred_element_type=jnp.float32)

    def up_term(first_row, row_count):
        partial_value = jnp.einsum(
            "slcf,ldf->slcd", grad_pre, w_in, preferred_element_type=jnp.float32
        )
        return partial_value.reshape(row_count, model_width)

    grad_slots = from_experts(up_term, sources * slot_rows)
    grad_routed = jnp.take(grad_slots, slot_of, axis=0).astype(jnp.float32)
    grad_norm_two, d_norm2_gain, d_norm2_bias = norm2_back(grad_routed)
    grad_residual = grad_out + grad_norm_two
    grad_joined = join_rows(grad_residual.astype(jnp.bfloat16))
    grad_heads = jnp.einsum(
        "td,hd->th", grad_joined, w_out, preferred_element_type=jnp.float32
    ).astype(jnp.bfloat16)
    d_w_out = jnp.einsum("th,td->hd", attn_out, grad_joined, preferred_element_type=jnp.float32)
    grad_seq = grad_heads.reshape(seq_count, length, heads_here, HD)

    def backward_pair(pair_index):
        query_block, key_seq, value_seq, first_row = pair_inputs(pair_index)
        grad_all = lax.dynamic_index_in_dim(grad_seq, pair_index // blocks, 0, keepdims=False)
        grad_block = lax.dynamic_slice_in_dim(grad_all, first_row, block_rows, 0)
        log_total = lax.dynamic_index_in_dim(log_totals, pair_index, 0, keepdims=False)
        return attend_back(
            query_block, key_seq, value_seq, grad_block, log_total, first_row, score_scale
        )

    grad_query, key_parts, value_parts = lax.map(
        backward_pair, jnp.arange(pair_count, dtype=jnp.int32)
    )
    head_width = heads_here * HD
    grad_query = grad_query.reshape(group_rows, head_width)
    grad_key = jnp.sum(key_parts.reshape(seq_count, blocks, length, head_width), axis=1).reshape(
        group_rows, head_width
    )
    grad_value = jnp.sum(
        value_parts.reshape(seq_count, blocks, length, head_width), axis=1
    ).reshape(group_rows, head_width)
    grad_qkv = jnp.stack([grad_query, grad_key, grad_value]).astype(jnp.bfloat16)
    d_w_qkv = jnp.einsum("td,ith->idh", joined, grad_qkv, preferred_element_type=jnp.float32)

    def qkv_term(first_row, row_count):
        return jnp.einsum("ith,idh->td", grad_qkv, w_qkv, preferred_element_type=jnp.float32)

    grad_normed = spread_rows(qkv_term, tok_rows)
    grad_norm_one, d_norm1_gain, d_norm1_bias = norm1_back(grad_normed)
    grad_input = grad_residual + grad_norm_one
    d_w_qkv, d_w_out = (
        lax.psum(d_w_qkv.astype(jnp.bfloat16), "exp").astype(jnp.float32),
        lax.psum(d_w_out.astype(jnp.bfloat16), "exp").astype(jnp.float32),
    )
    d_norm1_gain, d_norm1_bias, d_norm2_gain, d_norm2_bias = lax.psum(
        (d_norm1_gain, d_norm1_bias, d_norm2_gain, d_norm2_bias), ("exp", "hid")
    )
    return (
        output,
        grad_input,
        d_norm1_gain,
        d_norm1_bias,
        d_w_qkv,
        d_w_out,
        d_norm2_gain,
        d_norm2_bias,
        d_w_in,
        d_w_down,
    )


def solution(mesh):
    in_specs = (
        P(("exp", "hid"), None),
        P(),
        P(),
        P(None, None, "hid"),
        P("hid", None),
        P(),
        P(),
        P("exp", None, "hid"),
        P("exp", "hid", None),
        P(("exp", "hid"), None),
        P(("exp", "hid"), None),
    )
    out_specs = (
        P(("exp", "hid"), None),
        P(("exp", "hid"), None),
        P(),
        P(),
        P(None, None, "hid"),
        P("hid", None),
        P(),
        P(),
        P("exp", None, "hid"),
        P("exp", "hid", None),
    )
    return jax.shard_map(
        on_device, mesh=mesh, in_specs=in_specs, out_specs=out_specs, check_vma=False
    )
```

profile of v0, /device:TPU:1, one launch (start us, length us, event | category | flops | bytes accessed | tf_op | source)
XLA Modules:
  0.0 677.9 jit_solution(5014345327361731453)
XLA Ops:
  12.1 34.2 %all-gather.5.cloned.1.call-done = bf16[1024,1024]{1,0:T(8,128)(2,1)} async-done(((bf16[256,1024]{1,0:T(8,128)(2,1)}), bf16[1024,1024]{1,0:T(8,128)(2,1)}) %all-gather.5.cloned.1.call-update) | async-done | bytes 2097168 | tf_op jit(solution)/shard_map/all_gather | solution.py:26
  46.3 3.4 fusion.98
  50.8 23.2 %while.30 = (s32[]{:T(128)}, bf16[2,512,4,64]{1,3,2,0:T(8,128)(2,1)S(1)}, f32[2,4,512]{2,1,0:T(4,128)S(1)}, s32[2]{0:T(128)S(1)}, bf16[1,1024,4,64]{1,3,2,0:T(8,...) while((s32[]{:T(128)}, ...), condition=%wide.region_5.6_spmd, body=%wide.region_2.5_spmd.sunk | while | flops 562690560 | bytes 28905780 | solution.py:149
  53.8 2.6 fusion.158
  58.7 3.7 fusion.160
  65.4 2.6 fusion.158
  70.3 3.7 fusion.160
  75.5 3.1 convolution_convert_fusion
  81.4 2.8 gather_fusion.2
  84.2 24.3 %reduce-scatter.5.cloned.1.call-done = bf16[256,1024]{1,0:T(8,128)(2,1)} async-done(((bf16[1024,1024]{1,0:T(8,128)(2,1)}), bf16[256,1024]{1,0:T(8,128)(2,1)}) %reduce-scatter.5.cloned.1.call-update) | async-done | bytes 524304 | tf_op jit(solution)/shard_map/reduce_scatter | solution.py:30
  112.7 2.8 gather_fusion
  115.4 2.7 broadcast_select_fusion
  118.2 24.7 %all_to_all.48 = bf16[32,16,1024]{2,1,0:T(8,128)(2,1)} all-to-all(bf16[32,16,1024]{2,1,0:T(8,128)(2,1)S(1)} %bitcast.238), channel_id=1, replica_groups=mesh['exp'=32,'hid'=4] {'exp'}, dimensions={0} | all-to-all | bytes 2097152 | tf_op jit(solution)/shard_map/all_to_all | solution.py:39
  142.9 22.0 %all_to_all.49 = bf16[32,16,1024]{2,1,0:T(8,128)(2,1)} all-to-all(bf16[32,16,1024]{2,1,0:T(8,128)(2,1)} %bitcast.237), channel_id=1, replica_groups=mesh['exp'=32,'hid'=4] {'exp'}, dimensions={0} | all-to-all | bytes 2097152 | tf_op jit(solution)/shard_map/all_to_all | solution.py:39
  165.0 22.2 %all-gather.7.cloned.1.call-done = bf16[2048,1024]{1,0:T(8,128)(2,1)} async-done(((bf16[512,1024]{1,0:T(8,128)(2,1)}), bf16[2048,1024]{1,0:T(8,128)(2,1)}) %all-gather.7.cloned.1.call-update) | async-done | bytes 4194320 | tf_op jit(solution)/shard_map/all_gather | solution.py:40
  187.1 14.4 %fusion.60 = f32[2,128,8,1024]{3,1,2,0:T(8,128)} fusion(bf16[2,1024,1024]{2,1,0:T(8,128)(2,1)} %param.26, bf16[128,2,8,1024]{3,2,1,0:T(8,128)(2,1)} %bitcast.254), kind=kOutput, calls=%fused_computation.80 | convolution fusion | flops 4294967296 | bytes 16777216 | tf_op jit(solution)/shard_map/slcd,ldf->slcf/dot_general | solution.py:177
  201.5 8.5 %convert_bitcast_fusion.1 = bf16[128,2,8,1024]{3,0,2,1:T(8,128)(2,1)S(1)} fusion(bf16[2,1024,1024]{2,1,0:T(8,128)(2,1)S(1)} %copy-done.31, f32[2,128,8,1024]{3,1,2,0:T(8,128)} %fusion.60), kind=kOutput, calls=%fused_computation.89 | convolution fusion | flops 4315938816 | bytes 16777216 | tf_op jit(solution)/shard_map/slcf,lfd->slcd/dot_general | solution.py:181
  210.1 15.3 %copy.31 = bf16[128,2,8,1024]{3,2,1,0:T(8,128)(2,1)} copy(bf16[128,2,8,1024]{3,0,2,1:T(8,128)(2,1)S(1)} %convert_bitcast_fusion.1) | data formatting | bytes 8388608 | tf_op jit(solution)/shard_map/convert_element_type | solution.py:46
  225.5 11.9 %all-gather.9.cloned.1.call-done = bf16[2048,1024]{1,0:T(8,128)(2,1)} async-done(((bf16[512,1024]{1,0:T(8,128)(2,1)}), bf16[2048,1024]{1,0:T(8,128)(2,1)}) %all-gather.9.cloned.1.call-update) | async-done | bytes 4194320 | tf_op jit(solution)/shard_map/all_gather | solution.py:40
  237.4 15.3 %fusion.53 = bf16[128,2,8,1024]{3,0,2,1:T(8,128)(2,1)S(1)} fusion(f32[2,128,8,1024]{3,1,2,0:T(8,128)} %fusion.60, bf16[2,1024,1024]{2,1,0:T(8,128)(2,1)} %param.27, bf16[128,2,8,1024]{3,2,1,0:T(8,128)(2,1)} %bitcast.256), kind=kOutput, calls=%fused_computation.69 | convolution fusion | flops 4336910336 | bytes 20971520 | tf_op jit(solution)/shard_map/slcd,lfd->slcf/dot_general | solution.py:192
  252.8 4.8 convert_bitcast_fusion
  257.6 4.3 copy.33
  261.9 25.6 %reduce-scatter.7.cloned.1.call-done = bf16[512,1024]{1,0:T(8,128)(2,1)} async-done(((bf16[2048,1024]{1,0:T(8,128)(2,1)}), bf16[512,1024]{1,0:T(8,128)(2,1)}) %reduce-scatter.7.cloned.1.call-update) | async-done | bytes 1048592 | tf_op jit(solution)/shard_map/reduce_scatter | solution.py:45
  287.6 7.7 %all-to-all-start.1 = ((bf16[32,16,1024]{2,1,0:T(8,128)(2,1)}), bf16[32,16,1024]{2,1,0:T(8,128)(2,1)}, u32[]{:S(2)}, u32[]{:S(2)}) async-start(bf16[32,16,1024]{2,1,0:T(8,128)(2,1)} %bitcast.248), calls=%async_computation.3 | async-start | bytes 2097152 | tf_op jit(solution)/shard_map/all_to_all | solution.py:51
  295.2 41.7 %reduce-scatter.9.cloned.1.call-done = bf16[512,1024]{1,0:T(8,128)(2,1)} async-done(((bf16[2048,1024]{1,0:T(8,128)(2,1)}), bf16[512,1024]{1,0:T(8,128)(2,1)}) %reduce-scatter.9.cloned.1.call-update) | async-done | bytes 1048592 | tf_op jit(solution)/shard_map/reduce_scatter | solution.py:45
  337.0 7.7 %all-to-all-start.3 = ((bf16[32,16,1024]{2,1,0:T(8,128)(2,1)}), bf16[32,16,1024]{2,1,0:T(8,128)(2,1)}, u32[]{:S(2)}, u32[]{:S(2)}) async-start(bf16[32,16,1024]{2,1,0:T(8,128)(2,1)} %bitcast.247), calls=%async_computation.6 | async-start | bytes 2097152 | tf_op jit(solution)/shard_map/all_to_all | solution.py:51
  344.8 3.8 gather_fusion.1
  348.5 13.4 %all-to-all-done.3 = bf16[32,16,1024]{2,1,0:T(8,128)(2,1)} async-done(((bf16[32,16,1024]{2,1,0:T(8,128)(2,1)}), bf16[32,16,1024]{2,1,0:T(8,128)(2,1)}, u32[]{:S(2)}, u32[]{:S(2)}) %all-to-all-start.3) | async-done | bytes 1048608 | tf_op jit(solution)/shard_map/all_to_all | solution.py:51
  361.9 3.7 gather_fusion.3
  368.0 2.7 fusion.127
  373.2 26.3 %all-gather.11.cloned.1.call-done = bf16[1024,1024]{1,0:T(8,128)(2,1)} async-done(((bf16[256,1024]{1,0:T(8,128)(2,1)}), bf16[1024,1024]{1,0:T(8,128)(2,1)}) %all-gather.11.cloned.1.call-update) | async-done | bytes 2097168 | tf_op jit(solution)/shard_map/all_gather | solution.py:26
  399.5 2.4 convolution_convert_fusion.2
  401.9 41.0 %while.31 = (s32[]{:T(128)}, bf16[2,512,4,64]{1,3,2,0:T(8,128)(2,1)S(1)}, f32[2,1024,4,64]{1,3,2,0:T(8,128)}, f32[2,1024,4,64]{1,3,2,0:T(8,128)}, s32[2]{0:T(128...) while((s32[]{:T(128)}, ...), condition=%wide.region_19.22_spmd, body=%wide.region_17.21_spmd.sunk | while | flops 1374550528 | bytes 103870952 | solution.py:225
  406.2 2.4 fusion.169
  410.6 4.7 multiply_reduce_fusion.3
  415.3 2.4 multiply_convert_fusion.2
  431.1 4.7 multiply_reduce_fusion.3
  435.8 2.4 multiply_convert_fusion.2
  451.9 3.1 convolution_convert_fusion.1
  455.1 5.2 fusion.95
  460.5 3.2 bitcast_convert_fusion
  463.7 11.8 %fusion.71 = f32[2,1024,1024]{2,1,0:T(8,128)} fusion(bf16[128,2,8,1024]{3,2,1,0:T(8,128)(2,1)} %bitcast.255, bf16[128,2,8,1024]{3,0,2,1:T(8,128)(2,1)} %copy-done.34), kind=kOutput, calls=%fused_computation.93 | convolution fusion | flops 4294967296 | bytes 16777216 | tf_op jit(solution)/shard_map/slcd,slcf->ldf/dot_general | solution.py:197
  475.6 15.7 %fusion.74 = f32[2,1024,1024]{2,1,0:T(8,128)} fusion(bf16[128,2,8,1024]{3,2,1,0:T(8,128)(2,1)S(1)} %bitcast.257, f32[2,128,8,1024]{3,1,2,0:T(8,128)} %fusion.60), kind=kOutput, calls=%fused_computation.94 | convolution fusion | flops 4313841664 | bytes 20971520 | tf_op jit(solution)/shard_map/slcf,slcd->lfd/dot_general | solution.py:194
  491.3 76.6 %all-reduce.4.cloned.1.call-done = (bf16[3,1024,256]{1,2,0:T(8,128)(2,1)}, bf16[256,1024]{1,0:T(8,128)(2,1)}) async-done(((bf16[3,1024,256]{1,2,0:T(8,128)(2,1)}, bf16[256,1024]{1,0:T(8,128)(2,1)}), (bf16[3,1024,256]{1,2,0:T(8,128)(2,1)}, bf16[256,1024]{1,0:T(8,128)(2,1)})) %all-reduce.4.cloned.1.call-update) | async-done | bytes 2097168 | tf_op jit(solution)/shard_map/psum | solution.py:246
  570.1 3.1 copy.42
  573.2 26.7 %reduce-scatter.11.cloned.1.call-done = bf16[256,1024]{1,0:T(8,128)(2,1)} async-done(((bf16[1024,1024]{1,0:T(8,128)(2,1)}), bf16[256,1024]{1,0:T(8,128)(2,1)}) %reduce-scatter.11.cloned.1.call-update) | async-done | bytes 524304 | tf_op jit(solution)/shard_map/reduce_scatter | solution.py:30
  603.0 65.3 %all-reduce = (f32[1024]{0:T(1024)}, f32[1024]{0:T(1024)}, f32[1024]{0:T(1024)}, f32[1024]{0:T(1024)}) all-reduce(f32[1024]{0:T(1024)S(1)} %get-tuple-element.258, f32[1024]{0:T(1024)S(1)} %get-tuple-element.261, f32[1024]{0:T(1024)S(1)} %copy-done.22, f32[1024]{0:T(1024)S(1)} %copy-done.23), channel_id=1, replica_groups=mesh['exp'=32,'hid'=4] {'exp','hid'}, use_global_device_ids=true, to_apply=%region_26.29 | all-reduce | flops 4096 | bytes 32768 | tf_op jit(solution)/shard_map/psum | solution.py:249
  668.3 2.9 add_add_fusion.2
  (172 shorter events, 58.2 us)
Async XLA Ops:
  7.2 39.1 %copy-start = (bf16[3,1024,256]{2,1,0:T(8,128)(2,1)S(1)}, bf16[3,1024,256]{2,1,0:T(8,128)(2,1)}, u32[]{:S(2)}) copy-start(bf16[3,1024,256]{2,1,0:T(8,128)(2,1)} %param.22) | copy-start | bytes 4718596
  7.2 39.1 %all-gather.5.cloned.1.call-start = ((), (), s32[]{:S(2)}) async-start(), calls=%async_computation.8 | async-start | bytes 2621440 | tf_op jit(solution)/shard_map/all_gather | solution.py:26
  8.5 37.7 %copy-start.19 = (f32[256]{0:T(256)}, f32[256]{0:T(256)S(1)}, u32[]{:S(2)}) copy-start(f32[256]{0:T(256)S(1)} %broadcast_multiply_fusion.1) | copy-start | bytes 3076
  9.9 36.4 %copy-start.26 = (f32[256]{0:T(256)}, f32[256]{0:T(256)S(1)}, u32[]{:S(2)}) copy-start(f32[256]{0:T(256)S(1)} %fusion.108) | copy-start | bytes 3076
  9.9 36.4 %copy-start.24 = (f32[256]{0:T(256)}, f32[256]{0:T(256)S(1)}, u32[]{:S(2)}) copy-start(f32[256]{0:T(256)S(1)} %fusion.121) | copy-start | bytes 3076
  12.1 96.5 %reduce-scatter.5.cloned.1.call-start = ((), (), s32[]{:S(2)}) async-start(), calls=%async_computation.9 | async-start | bytes 2621440 | tf_op jit(solution)/shard_map/reduce_scatter | solution.py:30
  74.0 4.7 copy-start.21
  74.0 7.4 %copy-start.1 = (bf16[256,1024]{1,0:T(8,128)(2,1)S(1)}, bf16[256,1024]{1,0:T(8,128)(2,1)}, u32[]{:S(2)}) copy-start(bf16[256,1024]{1,0:T(8,128)(2,1)} %param.29) | copy-start | bytes 1572868
  78.6 108.5 %all-gather.7.cloned.1.call-start = ((), (), s32[]{:S(2)}) async-start(), calls=%async_computation.10 | async-start | bytes 5242880 | tf_op jit(solution)/shard_map/all_gather | solution.py:40
  81.4 27.1 %copy-start.3 = (bf16[256,1024]{1,0:T(8,128)(2,1)S(1)}, bf16[256,1024]{1,0:T(8,128)(2,1)}, u32[]{:S(2)}) copy-start(bf16[256,1024]{1,0:T(8,128)(2,1)} %param.19) | copy-start | bytes 1572868
  81.4 29.7 %copy-start.18 = (f32[1024]{0:T(1024)S(1)}, f32[1024]{0:T(1024)}, u32[]{:S(2)}) copy-start(f32[1024]{0:T(1024)} %param.24) | copy-start | bytes 12292
  81.4 29.7 %copy-start.30 = (f32[1024]{0:T(1024)S(1)}, f32[1024]{0:T(1024)}, u32[]{:S(2)}) copy-start(f32[1024]{0:T(1024)} %param.25) | copy-start | bytes 12292
  142.9 94.5 %all-gather.9.cloned.1.call-start = ((), (), s32[]{:S(2)}) async-start(), calls=%async_computation.12 | async-start | bytes 5242880 | tf_op jit(solution)/shard_map/all_gather | solution.py:40
  164.9 122.6 %reduce-scatter.7.cloned.1.call-start = ((), (), s32[]{:S(2)}) async-start(), calls=%async_computation.11 | async-start | bytes 5242880 | tf_op jit(solution)/shard_map/reduce_scatter | solution.py:45
  187.1 14.4 %copy-start.31 = (bf16[2,1024,1024]{2,1,0:T(8,128)(2,1)S(1)}, bf16[2,1024,1024]{2,1,0:T(8,128)(2,1)}, u32[]{:S(2)}) copy-start(bf16[2,1024,1024]{2,1,0:T(8,128)(2,1)} %param.27) | copy-start | bytes 12582916
  225.4 111.5 %reduce-scatter.9.cloned.1.call-start = ((), (), s32[]{:S(2)}) async-start(), calls=%async_computation.13 | async-start | bytes 5242880 | tf_op jit(solution)/shard_map/reduce_scatter | solution.py:45
  237.4 15.3 %copy-start.32 = (bf16[2,1024,1024]{2,1,0:T(8,128)(2,1)S(1)}, bf16[2,1024,1024]{2,1,0:T(8,128)(2,1)}, u32[]{:S(2)}) copy-start(bf16[2,1024,1024]{2,1,0:T(8,128)(2,1)} %param.26) | copy-start | bytes 12582916
  252.7 4.8 copy-start.34
  287.6 49.4 %all-to-all-start.1 = ((bf16[32,16,1024]{2,1,0:T(8,128)(2,1)}), bf16[32,16,1024]{2,1,0:T(8,128)(2,1)}, u32[]{:S(2)}, u32[]{:S(2)}) async-start(bf16[32,16,1024]{2,1,0:T(8,128)(2,1)} %bitcast.248), calls=%async_computation.3 | async-start | bytes 2097152 | tf_op jit(solution)/shard_map/all_to_all | solution.py:51
  337.0 24.9 %all-to-all-start.3 = ((bf16[32,16,1024]{2,1,0:T(8,128)(2,1)}), bf16[32,16,1024]{2,1,0:T(8,128)(2,1)}, u32[]{:S(2)}, u32[]{:S(2)}) async-start(bf16[32,16,1024]{2,1,0:T(8,128)(2,1)} %bitcast.247), calls=%async_computation.6 | async-start | bytes 2097152 | tf_op jit(solution)/shard_map/all_to_all | solution.py:51
  344.7 54.8 %all-gather.11.cloned.1.call-start = ((), (), s32[]{:S(2)}) async-start(), calls=%async_computation.14 | async-start | bytes 2621440 | tf_op jit(solution)/shard_map/all_gather | solution.py:26
  344.7 20.9 %copy-start.4 = (bf16[256,1024]{1,0:T(8,128)(2,1)S(1)}, bf16[256,1024]{1,0:T(8,128)(2,1)}, u32[]{:S(2)}) copy-start(bf16[256,1024]{1,0:T(8,128)(2,1)} %param.19) | copy-start | bytes 1572868
  370.7 2.4 copy-start.28
  372.7 195.3 %all-reduce.4.cloned.1.call-start = ((), (), s32[]{:S(2)}) async-start(), calls=%async_computation.16 | async-start | bytes 4194304 | tf_op jit(solution)/shard_map/psum | solution.py:246
  406.2 2.4 copy-start.7
  410.6 4.7 copy-start.8
  417.7 1.6 copy-start.9
  421.1 1.3 copy-start.10
  426.7 2.4 copy-start.7
  431.1 4.7 copy-start.8
  438.2 1.6 copy-start.9
  441.6 1.3 copy-start.10
  442.9 2.0 copy-start.14
  444.9 7.0 %copy-start.12 = (bf16[32,8,2,512]{3,1,2,0:T(8,128)(2,1)S(1)}, bf16[32,8,2,512]{3,1,2,0:T(8,128)(2,1)}, u32[]{:S(2)}) copy-start(bf16[32,8,2,512]{3,1,2,0:T(8,128)(2,1)} %copy-done.11) | copy-start | bytes 1572868
  455.1 5.4 copy-start.13
  455.1 5.4 copy-start.15
  455.1 5.4 copy-start.16
  460.3 139.6 %reduce-scatter.11.cloned.1.call-start = ((), (), s32[]{:S(2)}) async-start(), calls=%async_computation.15 | async-start | bytes 2621440 | tf_op jit(solution)/shard_map/reduce_scatter | solution.py:30
  463.7 11.9 %copy-start.33 = (bf16[2048,1024]{1,0:T(8,128)(2,1)S(1)}, bf16[2048,1024]{1,0:T(8,128)(2,1)}, u32[]{:S(2)}) copy-start(bf16[2048,1024]{1,0:T(8,128)(2,1)} %all-gather.9.cloned.1.call-done) | copy-start | bytes 12582916
  491.3 108.6 %copy-start.5 = (bf16[256,1024]{1,0:T(8,128)(2,1)S(1)}, bf16[256,1024]{1,0:T(8,128)(2,1)}, u32[]{:S(2)}) copy-start(bf16[256,1024]{1,0:T(8,128)(2,1)} %param.19) | copy-start | bytes 1572868
  491.3 108.6 %copy-start.17 = (f32[1024]{0:T(1024)S(1)}, f32[1024]{0:T(1024)}, u32[]{:S(2)}) copy-start(f32[1024]{0:T(1024)} %param.20) | copy-start | bytes 12292
  491.3 108.6 %copy-start.20 = (f32[256]{0:T(256)S(1)}, f32[256]{0:T(256)}, u32[]{:S(2)}) copy-start(f32[256]{0:T(256)} %copy-done.19) | copy-start | bytes 3076
  491.3 110.0 %copy-start.27 = (f32[256]{0:T(256)S(1)}, f32[256]{0:T(256)}, u32[]{:S(2)}) copy-start(f32[256]{0:T(256)} %copy-done.26) | copy-start | bytes 3076
  491.3 110.0 %copy-start.25 = (f32[256]{0:T(256)S(1)}, f32[256]{0:T(256)}, u32[]{:S(2)}) copy-start(f32[256]{0:T(256)} %copy-done.24) | copy-start | bytes 3076
  568.0 35.0 %copy-start.22 = (f32[1024]{0:T(1024)S(1)}, f32[1024]{0:T(1024)}, u32[]{:S(2)}) copy-start(f32[1024]{0:T(1024)} %get-tuple-element.256) | copy-start | bytes 12292
  568.0 35.0 %copy-start.23 = (f32[1024]{0:T(1024)S(1)}, f32[1024]{0:T(1024)}, u32[]{:S(2)}) copy-start(f32[1024]{0:T(1024)} %get-tuple-element.260) | copy-start | bytes 12292
  568.0 100.3 %copy-start.2 = (bf16[256,1024]{1,0:T(8,128)(2,1)S(1)}, bf16[256,1024]{1,0:T(8,128)(2,1)}, u32[]{:S(2)}) copy-start(bf16[256,1024]{1,0:T(8,128)(2,1)} %param.29) | copy-start | bytes 1572868
  568.0 100.3 %copy-start.29 = (f32[256]{0:T(256)S(1)}, f32[256]{0:T(256)}, u32[]{:S(2)}) copy-start(f32[256]{0:T(256)} %copy-done.28) | copy-start | bytes 3076
  (2 other events, 1.8 us)
Sparse Core Ops, SparseCore 0:
  12.2 34.0 all-gather.4
  78.8 29.7 reduce-scatter.4
  143.0 44.0 all-gather.6
  188.7 48.5 all-gather.8
  240.3 47.1 reduce-scatter.6
  290.4 46.5 reduce-scatter.8
  372.8 26.6 all-gather.10
  460.4 107.5 all-reduce.3
  570.5 29.3 reduce-scatter.10
where the time goes:
time: 687 us; the launch traced here: 678 us
  waiting for transfers between devices  303 us (44%)
  matrix products  128 us (19%)
  blocking collectives  112 us (16%)
  local copies, waits for them, and re-layouts  51.7 us (8%)
  other arithmetic  41.5 us (6%)
  starting transfers between devices  16.3 us (2%)
  between operations  14.6 us (2%)
  loops' own time  10.7 us (2%)
    psum x1, waiting for transfers between devices, on_device(): lax.psum(d_w_qkv.astype(jnp.bfloat16), 'exp').astype(jnp.float32)  76.6 us
    reduce_scatter x2, waiting for transfers between devices, from_experts(): lax.psum_scatter(term_of(jnp.int32(0), total_rows // hid_size * lax.axis_...  67.4 us
    psum x1, blocking collectives, on_device(): lax.psum((d_norm1_gain, d_norm1_bias, d_norm2_gain, d_norm2_bias), ('exp'...  65.3 us
    all_gather x2, waiting for transfers between devices, join_rows(): return lax.all_gather(token_rows, 'hid', axis=0, tiled=True)  60.5 us
    reduce_scatter x2, waiting for transfers between devices, spread_rows(): lax.psum_scatter(term_of(jnp.int32(0), own_rows * lax.axis_size('hid')).a...  51 us
    all_to_all x2, blocking collectives, to_experts(): lax.all_to_all(buffer, 'exp', split_axis=0, concat_axis=0, tiled=True)  46.7 us
    all_gather x2, waiting for transfers between devices, to_experts(): return lax.all_gather(arrived, 'hid', axis=0, tiled=True)  34.1 us
    convert_element_type x2, local copies, waits for them, and re-layouts, from_experts(): term_of(jnp.int32(0), total_rows // hid_size * lax.axis_size('hid'))  19.7 us
  transfers between devices with their start and end apart: 11, of which 10 were waited for; matrix products, arithmetic and copies ran while one was open for 16% of the time, Pallas kernels for 0%

commit v1 on v0

v1 whole, which is shorter than its diff:
```python
import jax
import jax.numpy as jnp
from jax import lax
from jax.experimental import pallas as pl
from jax.experimental.pallas import tpu as pltpu
from jax.sharding import PartitionSpec as P

HD = 64
EPSILON = 1e-05
NEG_LARGE = -1e30
BF = jnp.bfloat16
F32 = jnp.float32
MESH = pl.DeviceIdType.MESH
ANY = pl.BlockSpec(memory_space=pl.ANY)
VMEM = pl.BlockSpec(memory_space=pltpu.VMEM)
N_HID = 4
N_EXP = 32
ROWS = 256
WIDTH = 1024
SLOTS = 512
MIB = 1 << 20


def dot(a, b):
    return jnp.dot(a, b, preferred_element_type=F32)


def dot_nt(a, b):
    return lax.dot_general(a, b, (((1,), (1,)), ((), ())), preferred_element_type=F32)


def dot_tn(a, b):
    return lax.dot_general(a, b, (((0,), (0,)), ((), ())), preferred_element_type=F32)


def place():
    return lax.axis_index("exp"), lax.axis_index("hid")


def hid_of(h, step):
    return lax.rem(h + step + N_HID, N_HID)


def exp_of(e, dz, dx, dc):
    z, x, c = e // 8, lax.rem(e // 2, 4), lax.rem(e, 2)
    return (lax.rem(z + dz, 4) * 4 + lax.rem(x + dx, 4)) * 2 + lax.rem(c + dc, 2)


def plane_steps(order):
    return [
        (dz, dx, dc)
        for dz in order
        for dx in (0, 1, 3, 2)
        for dc in (0, 1)
        if (dz, dx, dc) != (0, 0, 0)
    ]


def greet(peers):
    barrier = pltpu.get_barrier_semaphore()
    for peer in peers:
        pl.semaphore_signal(barrier, inc=1, device_id=peer, device_id_type=MESH)
    pl.semaphore_wait(barrier, len(peers))


class Links:
    def __init__(self, send_sem, recv_sem):
        self.send_sem, self.recv_sem, self.used = send_sem, recv_sem, 0

    def remote(self, src, dst, peer):
        i = self.used
        self.used += 1
        copy = pltpu.make_async_remote_copy(
            src_ref=src,
            dst_ref=dst,
            send_sem=self.send_sem.at[i],
            recv_sem=self.recv_sem.at[i],
            device_id=peer,
            device_id_type=MESH,
        )
        copy.start()
        return copy

    def local(self, src, dst):
        i = self.used
        self.used += 1
        copy = pltpu.make_async_copy(src, dst, self.send_sem.at[i])
        copy.start()
        return copy


def rows_at(start, size, unit=16):
    return pl.ds(pl.multiple_of(start, unit), size)


def split_experts(block):
    n = block.shape[0] // 16
    wide = block.astype(F32).reshape(n, 2, 8, block.shape[1])
    return [wide[:, i].reshape(n * 8, block.shape[1]).astype(BF) for i in (0, 1)]


def merge_experts(first, second):
    n, width = first.shape[0] // 8, first.shape[1]
    pair = jnp.concatenate(
        [first.reshape(n, 1, 8, width), second.reshape(n, 1, 8, width)], axis=1
    )
    return pair.reshape(n * 16, width).astype(BF)


def norm_parts(rows):
    centered = rows - jnp.mean(rows, -1, keepdims=True)
    scale = lax.rsqrt(jnp.mean(centered * centered, -1, keepdims=True) + EPSILON)
    return centered * scale, scale


def norm_back(grad, hat, scale, gain):
    gh = grad * gain
    inner = jnp.mean(gh * hat, -1, keepdims=True)
    return scale * (gh - jnp.mean(gh, -1, keepdims=True) - hat * inner)


def start_kernel(x_ref, gain_ref, bias_ref, ids_ref, grad_ref, normed_ref, pick_ref, send_ref):
    hat, _ = norm_parts(x_ref[...].astype(F32))
    normed_ref[...] = (hat * gain_ref[...] + bias_ref[...]).astype(BF)
    ids = ids_ref[...]
    named = jnp.where(ids == lax.broadcasted_iota(jnp.int32, (ROWS, 128), 1), 1.0, 0.0)
    earlier = jnp.where(
        lax.broadcasted_iota(jnp.int32, (ROWS, ROWS), 1)
        < lax.broadcasted_iota(jnp.int32, (ROWS, ROWS), 0),
        1.0,
        0.0,
    )
    running = dot(earlier.astype(BF), named.astype(BF))
    position = jnp.sum(running * named, axis=1, keepdims=True).astype(jnp.int32)
    slot = ids * 8 + position
    pick = jnp.where(slot == lax.broadcasted_iota(jnp.int32, (ROWS, SLOTS), 1), 1.0, 0.0).astype(BF)
    pick_ref[...] = pick
    send_ref[...] = dot_tn(pick, grad_ref[...]).astype(BF)


def start_call(block_input, gain, bias, ids, out_grad):
    return pl.pallas_call(
        start_kernel,
        out_shape=(
            jax.ShapeDtypeStruct((ROWS, WIDTH), BF),
            jax.ShapeDtypeStruct((ROWS, SLOTS), BF),
            jax.ShapeDtypeStruct((SLOTS, WIDTH), BF),
        ),
        in_specs=[VMEM] * 5,
        out_specs=[VMEM] * 3,
        compiler_params=pltpu.CompilerParams(vmem_limit_bytes=32 * MIB),
        cost_estimate=pl.CostEstimate(flops=4 * 10**8, bytes_accessed=4 * MIB, transcendentals=0),
        name="start",
    )(block_input, gain, bias, ids, out_grad)


def gather_begin(links, src, out, e, h):
    up, down = (e, hid_of(h, 1)), (e, hid_of(h, -1))
    mine = out.at[rows_at(h * ROWS, ROWS)]
    first = links.remote(src, mine, up)
    second = links.remote(src, mine, down)
    return first, second, links.local(src, mine)


def gather_relay(links, begun, out, e, h):
    up, down = (e, hid_of(h, 1)), (e, hid_of(h, -1))
    half = ROWS // 2
    first, second, own = begun
    first.wait_recv()
    piece = out.at[rows_at(hid_of(h, -1) * ROWS, half)]
    third = links.remote(piece, piece, up)
    second.wait_recv()
    piece = out.at[rows_at(hid_of(h, 1) * ROWS + half, half)]
    fourth = links.remote(piece, piece, down)
    return first, second, third, fourth, own


def gather_end(copies):
    first, second, third, fourth, own = copies
    own.wait()
    third.wait()
    fourth.wait()
    first.wait_send()
    second.wait_send()


def reduce_begin(links, term, got, half_up, half_down, e, h):
    up, down = (e, hid_of(h, 1)), (e, hid_of(h, -1))
    half = ROWS // 2
    far, above, below = hid_of(h, 2) * ROWS, hid_of(h, 1) * ROWS, hid_of(h, -1) * ROWS
    one = links.remote(term.at[rows_at(far, half)], half_up, up)
    two = links.remote(term.at[rows_at(far + half, half)], half_down, down)
    three = links.remote(term.at[rows_at(above + half, half)], got.at[0, pl.ds(half, half)], up)
    four = links.remote(term.at[rows_at(below, half)], got.at[1, pl.ds(0, half)], down)
    return one, two, three, four


def reduce_middle(links, begun, term, got, half_up, half_down, pass_up, pass_down, e, h):
    up, down = (e, hid_of(h, 1)), (e, hid_of(h, -1))
    half = ROWS // 2
    above, below = hid_of(h, 1) * ROWS, hid_of(h, -1) * ROWS
    one, two, three, four = begun
    one.wait_recv()
    pass_up[...] = (
        term[rows_at(above, half), :].astype(F32) + half_up[...].astype(F32)
    ).astype(BF)
    five = links.remote(pass_up, got.at[0, pl.ds(0, half)], up)
    two.wait_recv()
    pass_down[...] = (
        term[rows_at(below + half, half), :].astype(F32) + half_down[...].astype(F32)
    ).astype(BF)
    six = links.remote(pass_down, got.at[1, pl.ds(half, half)], down)
    return one, two, three, four, five, six


def reduce_end(copies, term, got, h):
    for copy in copies[2:]:
        copy.wait_recv()
    return (
        term[rows_at(h * ROWS, ROWS), :].astype(F32)
        + got[0].astype(F32)
        + got[1].astype(F32)
    )


def reduce_scratch():
    half = ROWS // 2
    return [pltpu.VMEM((2, ROWS, WIDTH), BF)] + [pltpu.VMEM((half, WIDTH), BF)] * 4


def sems(count):
    return [pltpu.SemaphoreType.DMA((count,)), pltpu.SemaphoreType.DMA((count,))]


def hid_peers(e, h):
    return [(e, hid_of(h, 1)), (e, hid_of(h, -1))]


def plane_peers(e, h):
    return [(exp_of(e, *step), h) for step in plane_steps((0, 1, 3, 2))]


def first_kernel(normed_ref, send_ref, joined_ref, rows_ref, landed, send_sem, recv_sem):
    e, h = place()
    greet(hid_peers(e, h) + plane_peers(e, h))
    links = Links(send_sem, recv_sem)
    begun = gather_begin(links, normed_ref, joined_ref, e, h)
    own = landed.at[rows_at(e * 16, 16)]
    copies = []
    for step in plane_steps((0, 1, 3, 2)):
        t = exp_of(e, *step)
        copies.append(links.remote(send_ref.at[rows_at(t * 16, 16)], own, (t, h)))
    kept = links.local(send_ref.at[rows_at(e * 16, 16)], own)
    relayed = gather_relay(links, begun, joined_ref, e, h)
    kept.wait()
    for copy in copies:
        copy.wait_recv()
    for i in range(4):
        pair = split_experts(landed[pl.ds(i * 128, 128), :])
        for j in (0, 1):
            rows_ref[j, pl.ds(i * 64, 64), :] = pair[j]
    gather_end(relayed)
    for copy in copies:
        copy.wait_send()


def first_call(normed, send):
    return pl.pallas_call(
        first_kernel,
        out_shape=(
            jax.ShapeDtypeStruct((N_HID * ROWS, WIDTH), BF),
            jax.ShapeDtypeStruct((2, ROWS, WIDTH), BF),
        ),
        in_specs=[VMEM] * 2,
        out_specs=[VMEM] * 2,
        scratch_shapes=[pltpu.VMEM((SLOTS, WIDTH), BF)] + sems(37),
        compiler_params=pltpu.CompilerParams(
            collective_id=1, has_side_effects=True, vmem_limit_bytes=32 * MIB
        ),
        cost_estimate=pl.CostEstimate(flops=0, bytes_accessed=40 * MIB, transcendentals=0),
        name="gather_and_send",
    )(normed, send)


def head_lanes(shape, head):
    return lax.broadcasted_iota(jnp.int32, shape, 1) // HD == head


def causal_tail(scores_t):
    keys, queries = scores_t.shape
    tail = scores_t[keys - queries :]
    allowed = lax.broadcasted_iota(jnp.int32, tail.shape, 0) <= lax.broadcasted_iota(
        jnp.int32, tail.shape, 1
    )
    tail = jnp.where(allowed, tail, NEG_LARGE)
    if keys == queries:
        return tail
    return jnp.concatenate([scores_t[: keys - queries], tail], axis=0)


def forward_kernel(joined_ref, wqkv_ref, wout_ref, q_ref, k_ref, v_ref, heads_ref, logs_ref, term_ref, total):
    rows = joined_ref[...]
    q_ref[...] = dot(rows, wqkv_ref[0]).astype(BF)
    k_ref[...] = dot(rows, wqkv_ref[1]).astype(BF)
    v_ref[...] = dot(rows, wqkv_ref[2]).astype(BF)
    width = q_ref.shape[1]
    logs_ref[...] = jnp.zeros_like(logs_ref)
    for block in range(rows.shape[0] // ROWS):
        keys = (block + 1) * ROWS
        here = pl.ds(block * ROWS, ROWS)
        total[...] = jnp.zeros_like(total)

        def head_step(head, carry, keys=keys, here=here):
            lanes = head_lanes((ROWS, width), head)
            query = jnp.where(lanes, q_ref[here, :] * BF(HD**-0.5), BF(0))
            scores = causal_tail(dot_nt(k_ref[pl.ds(0, keys), :], query))
            top = jnp.max(scores, axis=0, keepdims=True)
            exps = jnp.exp(scores - top)
            summed = jnp.sum(exps, axis=0, keepdims=True)
            logs_ref[pl.ds(head, 1), here] = top + jnp.log(summed)
            probs = (exps * (1.0 / summed)).astype(BF)
            mixed = dot_tn(probs, v_ref[pl.ds(0, keys), :])
            total[...] = jnp.where(lanes, mixed, total[...])
            return carry

        lax.fori_loop(0, width // HD, head_step, 0)
        heads_ref[here, :] = total[...].astype(BF)
    term_ref[...] = dot(heads_ref[...], wout_ref[...]).astype(BF)


def forward_call(joined, w_qkv, w_out):
    rows, width = joined.shape[0], w_qkv.shape[2]
    part = jax.ShapeDtypeStruct((rows, width), BF)
    return pl.pallas_call(
        forward_kernel,
        out_shape=(part, part, part, part, jax.ShapeDtypeStruct((8, rows), F32), jax.ShapeDtypeStruct((rows, WIDTH), BF)),
        in_specs=[VMEM] * 3,
        out_specs=[VMEM] * 6,
        scratch_shapes=[pltpu.VMEM((ROWS, width), F32)],
        compiler_params=pltpu.CompilerParams(vmem_limit_bytes=48 * MIB),
        cost_estimate=pl.CostEstimate(flops=6 * 10**9, bytes_accessed=8 * MIB, transcendentals=4 * 10**6),
        name="attention_forward",
    )(joined, w_qkv, w_out)


def second_kernel(
    term_ref, x_ref, gain_ref, bias_ref, pick_ref,
    residual_ref, rows_ref,
    got, half_up, half_down, pass_up, pass_down, outgoing, landed, staged, send_sem, recv_sem,
):
    e, h = place()
    up, down = (e, hid_of(h, 1)), (e, hid_of(h, -1))
    z = e // 8
    greet(hid_peers(e, h) + plane_peers(e, h))
    links = Links(send_sem, recv_sem)
    begun = reduce_begin(links, term_ref, got, half_up, half_down, e, h)
    reduced = reduce_middle(links, begun, term_ref, got, half_up, half_down, pass_up, pass_down, e, h)
    residual = x_ref[...].astype(F32) + reduce_end(reduced, term_ref, got, h)
    residual_ref[...] = residual
    hat, _ = norm_parts(residual)
    routed = (hat * gain_ref[...] + bias_ref[...]).astype(BF)
    outgoing[...] = dot_tn(pick_ref[...], routed).astype(BF)
    mine = landed.at[rows_at(e * 16, 16)]
    order = (0, 1, 3, 2)
    sent = {}
    for dz in order:
        sent[dz] = []
        for step in plane_steps((dz,)):
            t = exp_of(e, *step)
            sent[dz].append(links.remote(outgoing.at[rows_at(t * 16, 16)], mine, (t, h)))
    kept = links.local(outgoing.at[rows_at(e * 16, 16)], mine)
    waits = []
    pending = None

    def relay(chunk):
        at, first, second = chunk
        first.wait_recv()
        third = links.remote(
            rows_ref.at[0, rows_at(ROWS + at, 64)], rows_ref.at[0, rows_at(3 * ROWS + at, 64)], up
        )
        second.wait_recv()
        fourth = links.remote(
            rows_ref.at[1, rows_at(2 * ROWS + at, 64)], rows_ref.at[1, rows_at(3 * ROWS + at, 64)], down
        )
        waits.extend((third, fourth))

    for dz in order:
        if dz == 0:
            kept.wait()
        for copy in sent[dz]:
            copy.wait_recv()
        from_z = lax.rem(z - dz + 4, 4)
        at = from_z * 64
        pair = split_experts(landed[rows_at(from_z * 128, 128), :])
        for j in (0, 1):
            staged[j, rows_at(at, 64), :] = pair[j]
        piece = staged.at[:, rows_at(at, 64)]
        first = links.remote(piece, rows_ref.at[:, rows_at(ROWS + at, 64)], up)
        second = links.remote(piece, rows_ref.at[:, rows_at(2 * ROWS + at, 64)], down)
        own = links.local(piece, rows_ref.at[:, rows_at(at, 64)])
        if pending is not None:
            relay(pending)
        pending = (at, first, second)
        waits.append(own)
        sent[dz].extend((first, second))
    relay(pending)
    for copy in waits:
        copy.wait()
    for dz in order:
        for copy in sent[dz]:
            copy.wait_send()
    for copy in reduced:
        copy.wait_send()


def second_call(term, block_input, gain, bias, pick):
    return pl.pallas_call(
        second_kernel,
        out_shape=(
            jax.ShapeDtypeStruct((ROWS, WIDTH), F32),
            jax.ShapeDtypeStruct((2, N_HID * ROWS, WIDTH), BF),
        ),
        in_specs=[VMEM] * 5,
        out_specs=[VMEM, ANY],
        scratch_shapes=reduce_scratch()
        + [pltpu.VMEM((SLOTS, WIDTH), BF)] * 2
        + [pltpu.VMEM((2, ROWS, WIDTH), BF)]
        + sems(6 + 32 + 20),
        compiler_params=pltpu.CompilerParams(
            collective_id=2, has_side_effects=True, vmem_limit_bytes=32 * MIB
        ),
        cost_estimate=pl.CostEstimate(flops=0, bytes_accessed=100 * MIB, transcendentals=0),
        name="reduce_norm_send",
    )(term, block_input, gain, bias, pick)


def expert_kernel(x_ref, g0_ref, g1_ref, g2_ref, g3a_ref, g3b_ref, win_ref, wdown_ref, act_ref, gpre_ref, up_ref, grad_ref):
    expert, block = pl.program_id(0), pl.program_id(1)
    for i, ref in enumerate((g0_ref, g1_ref, g2_ref)):

        @pl.when(block == i)
        def _(ref=ref):
            grad_ref[...] = ref[...]

    for i, ref in enumerate((g3a_ref, g3b_ref)):

        @pl.when((block == 3) & (expert == i))
        def _(ref=ref):
            grad_ref[0] = ref[...]

    pre = dot(x_ref[0], win_ref[0])
    grad_act = dot_nt(grad_ref[0], wdown_ref[0])
    root = 0.7978845608028654
    square = pre * pre
    curve = jnp.tanh(root * (pre + 0.044715 * (square * pre)))
    half = 0.5 * (1.0 + curve)
    act_ref[0] = (pre * half).astype(BF)
    slope = half + 0.5 * pre * (1.0 - curve * curve) * (root * (1.0 + 3 * 0.044715 * square))
    grad_pre = (grad_act * slope).astype(BF)
    gpre_ref[0] = grad_pre
    up_ref[0] = dot_nt(grad_pre, win_ref[0]).astype(BF)


def expert_call(rows, grads, w_in, w_down):
    whole = jax.ShapeDtypeStruct(rows.shape, BF)
    part = pl.BlockSpec((1, ROWS, WIDTH), lambda i, j: (i, j, 0))
    fixed = pl.BlockSpec((1, ROWS, WIDTH), lambda i, j: (i, 0, 0))
    weight = pl.BlockSpec((1, WIDTH, WIDTH), lambda i, j: (i, 0, 0))
    flat = pl.BlockSpec((ROWS, WIDTH), lambda i, j: (0, 0))
    return pl.pallas_call(
        expert_kernel,
        grid=(2, N_HID),
        out_shape=(whole,) * 4,
        in_specs=[part, fixed, fixed, fixed, flat, flat, weight, weight],
        out_specs=[part] * 4,
        compiler_params=pltpu.CompilerParams(vmem_limit_bytes=48 * MIB),
        cost_estimate=pl.CostEstimate(flops=13 * 10**9, bytes_accessed=32 * MIB, transcendentals=2 * 10**6),
        name="experts",
    )(rows, *grads, w_in, w_down)


def third_kernel(
    up_ref, pick_ref, residual_ref, grad_ref, gain_ref,
    gres_ref, joined_ref, vec_ref,
    ub, half_up, half_down, pass_up, pass_down, got, outgoing, landed, gradient, send_sem, recv_sem,
):
    e, h = place()
    up, down = (e, hid_of(h, 1)), (e, hid_of(h, -1))
    z = e // 8
    greet(hid_peers(e, h) + plane_peers(e, h))
    links = Links(send_sem, recv_sem)
    order = (2, 1, 3, 0)
    begun = []
    for dz in order:
        at = lax.rem(z + dz, 4) * 64
        piece = rows_at(at, 64)
        far, above, below = (rows_at(k * ROWS + at, 64) for k in (3, 2, 1))
        begun.append((
            at,
            links.remote(up_ref.at[0, far], half_up.at[piece], up),
            links.remote(up_ref.at[1, far], half_down.at[piece], down),
            links.remote(up_ref.at[1, above], got.at[0, 1, piece], up),
            links.remote(up_ref.at[0, below], got.at[1, 0, piece], down),
        ))
    held = links.local(up_ref.at[:, pl.ds(0, 3 * ROWS)], ub)
    held.wait()
    passed = []
    for at, one, two, three, four in begun:
        piece = rows_at(at, 64)
        one.wait_recv()
        pass_up[piece, :] = (
            ub[0, rows_at(2 * ROWS + at, 64), :].astype(F32) + half_up[piece, :].astype(F32)
        ).astype(BF)
        five = links.remote(pass_up.at[piece], got.at[0, 0, piece], up)
        two.wait_recv()
        pass_down[piece, :] = (
            ub[1, rows_at(ROWS + at, 64), :].astype(F32) + half_down[piece, :].astype(F32)
        ).astype(BF)
        six = links.remote(pass_down.at[piece], got.at[1, 1, piece], down)
        passed.append((five, six))
    mine = landed.at[rows_at(e * 16, 16)]
    back = []
    for dz, (at, one, two, three, four), (five, six) in zip(order, begun, passed):
        for copy in (three, four, five, six):
            copy.wait_recv()
        piece = rows_at(at, 64)
        pair = [
            ub[j, piece, :].astype(F32) + got[0, j, piece, :].astype(F32) + got[1, j, piece, :].astype(F32)
            for j in (0, 1)
        ]
        outgoing[rows_at(at * 2, 128), :] = merge_experts(*pair)
        for step in plane_steps((dz,)):
            t = exp_of(e, *step)
            back.append(links.remote(outgoing.at[rows_at(t * 16, 16)], mine, (t, h)))
    kept = links.local(outgoing.at[rows_at(e * 16, 16)], mine)
    kept.wait()
    for copy in back:
        copy.wait_recv()
    routed = dot(pick_ref[...], landed[...])
    hat, scale = norm_parts(residual_ref[...])
    vec_ref[...] = jnp.zeros_like(vec_ref)
    vec_ref[2:3, :] = jnp.sum(routed * hat, axis=0, keepdims=True)
    vec_ref[3:4, :] = jnp.sum(routed, axis=0, keepdims=True)
    gres = grad_ref[...].astype(F32) + norm_back(routed, hat, scale, gain_ref[...])
    gres_ref[...] = gres
    gradient[...] = gres.astype(BF)
    gathered = gather_relay(links, gather_begin(links, gradient, joined_ref, e, h), joined_ref, e, h)
    gather_end(gathered)
    for copy in back:
        copy.wait_send()
    for _, *copies in begun:
        for copy in copies:
            copy.wait_send()
    for pair in passed:
        for copy in pair:
            copy.wait_send()


def third_call(up, pick, residual, out_grad, gain):
    full = pltpu.VMEM((ROWS, WIDTH), BF)
    return pl.pallas_call(
        third_kernel,
        out_shape=(
            jax.ShapeDtypeStruct((ROWS, WIDTH), F32),
            jax.ShapeDtypeStruct((N_HID * ROWS, WIDTH), BF),
            jax.ShapeDtypeStruct((8, WIDTH), F32),
        ),
        in_specs=[ANY] + [VMEM] * 4,
        out_specs=[VMEM] * 3,
        scratch_shapes=[pltpu.VMEM((2, 3 * ROWS, WIDTH), BF)]
        + [full] * 4
        + [pltpu.VMEM((2, 2, ROWS, WIDTH), BF)]
        + [pltpu.VMEM((SLOTS, WIDTH), BF)] * 2
        + [full]
        + sems(16 + 8 + 1 + 32 + 5),
        compiler_params=pltpu.CompilerParams(
            collective_id=3, has_side_effects=True, vmem_limit_bytes=40 * MIB
        ),
        cost_estimate=pl.CostEstimate(flops=0, bytes_accessed=100 * MIB, transcendentals=0),
        name="reduce_back_gather",
    )(up, pick, residual, out_grad, gain)


def backward_kernel(
    grad_ref, wout_ref, wqkv_ref, joined_ref, q_ref, k_ref, v_ref, heads_ref, logs_ref,
    term_ref, dw_ref,
    gheads, gq, gk, gv, dq,
):
    rows, width = q_ref.shape
    gheads[...] = dot_nt(grad_ref[...], wout_ref[...]).astype(BF)
    for i in range(4):
        block = dot_tn(heads_ref[...], grad_ref[:, pl.ds(i * width, width)])
        dw_ref[pl.ds(3 * WIDTH + i * width, width), :] = block.astype(BF)
    gk[...] = jnp.zeros_like(gk)
    gv[...] = jnp.zeros_like(gv)
    for block in range(rows // ROWS):
        keys = (block + 1) * ROWS
        here = pl.ds(block * ROWS, ROWS)
        dq[...] = jnp.zeros_like(dq)

        def head_step(head, carry, keys=keys, here=here):
            lanes = head_lanes((ROWS, width), head)
            query = jnp.where(lanes, q_ref[here, :] * BF(HD**-0.5), BF(0))
            grad = jnp.where(lanes, gheads[here, :], BF(0))
            scores = causal_tail(dot_nt(k_ref[pl.ds(0, keys), :], query))
            probs = jnp.exp(scores - logs_ref[pl.ds(head, 1), here])
            weighted = probs * dot_nt(v_ref[pl.ds(0, keys), :], grad)
            inner = jnp.sum(weighted, axis=0, keepdims=True)
            grad_scores = (weighted - probs * inner).astype(BF)
            gv[pl.ds(0, keys), :] += dot(probs.astype(BF), grad)
            gk[pl.ds(0, keys), :] += dot(grad_scores, query)
            dq[...] = jnp.where(lanes, dot_tn(grad_scores, k_ref[pl.ds(0, keys), :]), dq[...])
            return carry

        lax.fori_loop(0, width // HD, head_step, 0)
        gq[here, :] = (dq[...] * HD**-0.5).astype(BF)
    parts = (gq[...], gk[...].astype(BF), gv[...].astype(BF))
    term_ref[...] = sum(dot_nt(part, wqkv_ref[i]) for i, part in enumerate(parts)).astype(BF)
    for i, part in enumerate(parts):
        dw_ref[pl.ds(i * WIDTH, WIDTH), :] = dot_tn(joined_ref[...], part).astype(BF)


def backward_call(grad, w_out, w_qkv, joined, q, k, v, heads, logs):
    rows, width = q.shape
    return pl.pallas_call(
        backward_kernel,
        out_shape=(
            jax.ShapeDtypeStruct((rows, WIDTH), BF),
            jax.ShapeDtypeStruct((4 * WIDTH, width), BF),
        ),
        in_specs=[VMEM] * 9,
        out_specs=[VMEM] * 2,
        scratch_shapes=[
            pltpu.VMEM((rows, width), BF),
            pltpu.VMEM((rows, width), BF),
            pltpu.VMEM((rows, width), F32),
            pltpu.VMEM((rows, width), F32),
            pltpu.VMEM((ROWS, width), F32),
        ],
        compiler_params=pltpu.CompilerParams(vmem_limit_bytes=52 * MIB),
        cost_estimate=pl.CostEstimate(flops=12 * 10**9, bytes_accessed=12 * MIB, transcendentals=4 * 10**6),
        name="attention_backward",
    )(grad, w_out, w_qkv, joined, q, k, v, heads, logs)


CHIPS = [(dz, dx, 0) for dz in (0, 1, 3, 2) for dx in (0, 1, 3, 2) if (dz, dx) != (0, 0)]


def last_kernel(
    term_ref, gres_ref, x_ref, gain_ref, mixed_ref, pick_ref, residual_ref, dw_ref, vec_ref,
    out_ref, ginput_ref, dwsum_ref, vecsum_ref,
    got, half_up, half_down, pass_up, pass_down, outgoing, landed,
    core_got, halves, pieces, summed, vec, vec_got, send_sem, recv_sem,
):
    e, h = place()
    z, x, c = e // 8, lax.rem(e // 2, 4), lax.rem(e, 2)
    chip = z * 4 + x
    twin = (exp_of(e, 0, 0, 1), h)
    across = [(exp_of(e, *step), h) for step in CHIPS]
    greet(hid_peers(e, h) + [(e, hid_of(h, 2))] + plane_peers(e, h))
    links = Links(send_sem, recv_sem)
    half = 2 * WIDTH
    swap = links.remote(dw_ref.at[rows_at((1 - c) * half, half)], core_got, twin)
    begun = reduce_begin(links, term_ref, got, half_up, half_down, e, h)
    mine = landed.at[rows_at(e * 16, 16)]
    back = []
    for i in range(4):
        pair = [mixed_ref[j, pl.ds(i * 64, 64), :].astype(F32) for j in (0, 1)]
        outgoing[pl.ds(i * 128, 128), :] = merge_experts(*pair)
    for step in plane_steps((2, 1, 3, 0)):
        t = exp_of(e, *step)
        back.append(links.remote(outgoing.at[rows_at(t * 16, 16)], mine, (t, h)))
    kept = links.local(outgoing.at[rows_at(e * 16, 16)], mine)
    swap.wait_recv()
    halves[...] = (
        dw_ref[rows_at(c * half, half), :].astype(F32) + core_got[...].astype(F32)
    ).astype(BF)
    spread = []
    for i, peer in enumerate(across):
        t = peer[0] // 2
        spread.append(links.remote(halves.at[rows_at(t * 128, 128)], pieces.at[i], peer))
    reduced = reduce_middle(links, begun, term_ref, got, half_up, half_down, pass_up, pass_down, e, h)
    grad = reduce_end(reduced, term_ref, got, h)
    hat, scale = norm_parts(x_ref[...].astype(F32))
    ginput_ref[...] = gres_ref[...] + norm_back(grad, hat, scale, gain_ref[...])
    vec[0] = vec_ref[...]
    vec[0, 0:1, :] = jnp.sum(grad * hat, axis=0, keepdims=True)
    vec[0, 1:2, :] = jnp.sum(grad, axis=0, keepdims=True)
    rounds = (
        [(e, hid_of(h, k)) for k in (1, 2, 3)],
        [(exp_of(e, 0, dx, dc), h) for dx in range(4) for dc in (0, 1) if (dx, dc) != (0, 0)],
        [(exp_of(e, dz, 0, 0), h) for dz in (1, 2, 3)],
    )
    small = []
    slot = 0
    copies = [links.remote(vec.at[0], vec_got.at[slot + i], peer) for i, peer in enumerate(rounds[0])]
    for copy in spread:
        copy.wait_recv()
    total = halves[rows_at(chip * 128, 128), :].astype(F32)
    for i in range(len(across)):
        total = total + pieces[i].astype(F32)
    summed[...] = total.astype(BF)
    place_of = dwsum_ref.at[rows_at(c * half + chip * 128, 128)]
    share = [links.remote(summed, place_of, peer) for peer in across]
    share_own = links.local(summed, place_of)
    for number in range(3):
        for copy in copies:
            copy.wait_recv()
        whole = vec[number]
        for i in range(len(rounds[number])):
            whole = whole + vec_got[slot + i]
        slot += len(rounds[number])
        small.extend(copies)
        if number < 2:
            vec[number + 1] = whole
            copies = [
                links.remote(vec.at[number + 1], vec_got.at[slot + i], peer)
                for i, peer in enumerate(rounds[number + 1])
            ]
        else:
            vecsum_ref[...] = whole
    kept.wait()
    for copy in back:
        copy.wait_recv()
    out_ref[...] = (residual_ref[...] + dot(pick_ref[...], landed[...])).astype(BF)
    share_own.wait()
    for copy in share:
        copy.wait_recv()
    both = dwsum_ref.at[rows_at(c * half, half)]
    twins = links.remote(both, both, twin)
    twins.wait()
    swap.wait_send()
    for copy in list(reduced) + back + spread + share + small:
        copy.wait_send()


def last_call(term, gres, block_input, gain, mixed, pick, residual, dw, vec):
    return pl.pallas_call(
        last_kernel,
        out_shape=(
            jax.ShapeDtypeStruct((ROWS, WIDTH), BF),
            jax.ShapeDtypeStruct((ROWS, WIDTH), F32),
            jax.ShapeDtypeStruct(dw.shape, BF),
            jax.ShapeDtypeStruct((8, WIDTH), F32),
        ),
        in_specs=[VMEM] * 9,
        out_specs=[VMEM] * 4,
        scratch_shapes=reduce_scratch()
        + [pltpu.VMEM((SLOTS, WIDTH), BF)] * 2
        + [
            pltpu.VMEM((2 * WIDTH, dw.shape[1]), BF),
            pltpu.VMEM((2 * WIDTH, dw.shape[1]), BF),
            pltpu.VMEM((15, 128, dw.shape[1]), BF),
            pltpu.VMEM((128, dw.shape[1]), BF),
            pltpu.VMEM((3, 8, WIDTH), F32),
            pltpu.VMEM((13, 8, WIDTH), F32),
        ]
        + sems(1 + 6 + 32 + 15 + 16 + 13 + 1),
        compiler_params=pltpu.CompilerParams(
            collective_id=4, has_side_effects=True, vmem_limit_bytes=48 * MIB
        ),
        cost_estimate=pl.CostEstimate(flops=0, bytes_accessed=100 * MIB, transcendentals=0),
        name="last_sums",
    )(term, gres, block_input, gain, mixed, pick, residual, dw, vec)


def hid_shift(rows, step):
    return lax.ppermute(rows, "hid", [(i, (i + step) % N_HID) for i in range(N_HID)])


def added(*terms):
    return sum(term.astype(F32) for term in terms).astype(BF)


def on_device(
    block_input, norm1_gain, norm1_bias, w_qkv, w_out, norm2_gain, norm2_bias,
    w_in, w_down, expert_ids, out_grad,
):
    gain1, bias1, gain2, bias2 = (
        v.reshape(1, WIDTH) for v in (norm1_gain, norm1_bias, norm2_gain, norm2_bias)
    )
    normed, pick, grad_send = start_call(block_input, gain1, bias1, expert_ids, out_grad)
    joined, g0 = first_call(normed, grad_send)
    g1 = hid_shift(g0, 1)
    g2 = hid_shift(g0, -1)
    g3a = hid_shift(g1[0], 1)
    g3b = hid_shift(g2[1], -1)
    q, k, v, heads, logs, term = forward_call(joined, w_qkv, w_out)
    residual, rows = second_call(term, block_input, gain2, bias2, pick)
    act, grad_pre, up, grads = expert_call(rows, (g0, g1, g2, g3a, g3b), w_in, w_down)
    gres, grad_joined, vec = third_call(up, pick, residual, out_grad, gain2)
    down = jnp.einsum("lrf,lfd->lrd", act, w_down, preferred_element_type=F32).astype(BF)
    blocks = [[down[j, i * ROWS : (i + 1) * ROWS] for i in range(4)] for j in (0, 1)]
    far_up = hid_shift(blocks[0][3], 1)
    far_down = hid_shift(blocks[1][3], -1)
    up1 = hid_shift(blocks[1][2], 1)
    down0 = hid_shift(blocks[0][1], -1)
    up0 = hid_shift(added(blocks[0][2], far_up), 1)
    down1 = hid_shift(added(blocks[1][1], far_down), -1)
    mixed = jnp.stack(
        [added(blocks[0][0], up0, down0), added(blocks[1][0], up1, down1)]
    )
    d_w_in = jnp.einsum("lrd,lrf->ldf", rows, grad_pre, preferred_element_type=F32)
    d_w_down = jnp.einsum("lrf,lrd->lfd", act, grads, preferred_element_type=F32)
    back_term, dw = backward_call(grad_joined, w_out, w_qkv, joined, q, k, v, heads, logs)
    output, grad_input, dw_sum, vec_sum = last_call(
        back_term, gres, block_input, gain1, mixed, pick, residual, dw, vec
    )
    width = w_qkv.shape[2]
    d_w_qkv = dw_sum[: 3 * WIDTH].reshape(3, WIDTH, width).astype(F32)
    d_w_out = (
        dw_sum[3 * WIDTH :].reshape(4, width, width).transpose(1, 0, 2).reshape(width, WIDTH).astype(F32)
    )
    return (
        output, grad_input, vec_sum[0], vec_sum[1], d_w_qkv, d_w_out,
        vec_sum[2], vec_sum[3], d_w_in, d_w_down,
    )


def solution(mesh):
    in_specs = (
        P(("exp", "hid"), None), P(), P(), P(None, None, "hid"), P("hid", None), P(), P(),
        P("exp", None, "hid"), P("exp", "hid", None), P(("exp", "hid"), None), P(("exp", "hid"), None),
    )
    out_specs = (
        P(("exp", "hid"), None), P(("exp", "hid"), None), P(), P(), P(None, None, "hid"), P("hid", None),
        P(), P(), P("exp", None, "hid"), P("exp", "hid", None),
    )
    return jax.shard_map(on_device, mesh=mesh, in_specs=in_specs, out_specs=out_specs, check_vma=False)
```

time: 687 us -> 400 us (0.58); the launches traced: 678 us -> 400 us
  Pallas kernels: 0 us -> 311 us
  waiting for transfers between devices: 303 us -> 28.7 us
  blocking collectives: 112 us -> 0 us
  matrix products: 128 us -> 22.9 us
  other arithmetic: 41.5 us -> 6.36 us
  local copies, waits for them, and re-layouts: 51.7 us -> 17.9 us
  between operations: 14.6 us -> 0.91 us
  loops' own time: 10.7 us -> 0 us
    pallas_call x0 -> x8, Pallas kernels: none -> 311 us  [the longest x1 84.1 us: third_call(): pl.pallas_call(third_kernel, out_shape=(jax.ShapeDtypeStruct((ROWS, WIDTH...]
    reduce_scatter x4 -> x0, waiting for transfers between devices: 118 us -> none  [the longest x2 67.4 us: from_experts(): lax.psum_scatter(term_of(jnp.int32(0), total_rows // hid_size * lax.axis_...]
    dot_general x26 -> x3, matrix products: 128 us -> 22.9 us  [the longest x1 9.16 us: on_device(): jnp.einsum('lrd,lrf->ldf', rows, grad_pre, preferred_element_type=F32)]
    all_gather x4 -> x0, waiting for transfers between devices: 94.5 us -> none  [the longest x2 60.5 us: join_rows(): return lax.all_gather(token_rows, 'hid', axis=0, tiled=True)]
    psum x1 -> x0, waiting for transfers between devices: 76.6 us -> none  [on_device(): lax.psum(d_w_qkv.astype(jnp.bfloat16), 'exp').astype(jnp.float32)]
    psum x1 -> x0, blocking collectives: 65.3 us -> none  [on_device(): lax.psum((d_norm1_gain, d_norm1_bias, d_norm2_gain, d_norm2_bias), ('exp'...]
    all_to_all x2 -> x0, blocking collectives: 46.7 us -> none  [to_experts(): lax.all_to_all(buffer, 'exp', split_axis=0, concat_axis=0, tiled=True)]
    ppermute x0 -> x10, waiting for transfers between devices: none -> 28.7 us  [hid_shift(): lax.ppermute(rows, 'hid', [(i, (i + step) % N_HID) for i in range(N_HID)])]
  transfers between devices with their start and end apart: 11 -> 10, of which waited for: 10 -> 3; matrix products, arithmetic and copies ran while one was open for 16% -> 5% of each run, Pallas kernels for 0% -> 48%
where the time goes in v1:
time: 400 us
  Pallas kernels  311 us (78%)
  waiting for transfers between devices  28.7 us (7%)
  matrix products  22.9 us (6%)
  local copies, waits for them, and re-layouts  17.9 us (4%)
  starting transfers between devices  11.8 us (3%)
  other arithmetic  6.36 us (2%)
    pallas_call x1, Pallas kernels, third_call(): pl.pallas_call(third_kernel, out_shape=(jax.ShapeDtypeStruct((ROWS, WIDTH...  84.1 us
    pallas_call x1, Pallas kernels, second_call(): pl.pallas_call(second_kernel, out_shape=(jax.ShapeDtypeStruct((ROWS, WIDT...  69 us
    pallas_call x1, Pallas kernels, last_call(): pl.pallas_call(last_kernel, out_shape=(jax.ShapeDtypeStruct((ROWS, WIDTH)...  65.9 us
    pallas_call x1, Pallas kernels, first_call(): pl.pallas_call(first_kernel, out_shape=(jax.ShapeDtypeStruct((N_HID * ROW...  29.6 us
    ppermute x10, waiting for transfers between devices, hid_shift(): lax.ppermute(rows, 'hid', [(i, (i + step) % N_HID) for i in range(N_HID)])  28.7 us
    pallas_call x1, Pallas kernels, backward_call(): pl.pallas_call(backward_kernel, out_shape=(jax.ShapeDtypeStruct((rows, WI...  22.4 us
    pallas_call x1, Pallas kernels, expert_call(): pl.pallas_call(expert_kernel, grid=(2, N_HID), out_shape=(whole,) * 4, in...  21 us
    pallas_call x1, Pallas kernels, forward_call(): pl.pallas_call(forward_kernel, out_shape=(part, part, part, part, jax.Sha...  18.3 us
  transfers between devices with their start and end apart: 10, of which 3 were waited for; matrix products, arithmetic and copies ran while one was open for 5% of the time, Pallas kernels for 48%

profile of v1, /device:TPU:1, one launch (start us, length us, event | category | flops | bytes accessed | tf_op | source)
XLA Modules:
  0.0 399.8 jit_solution(4858373124825493210)
XLA Ops:
  0.6 0.8 copy.21.ids_ref
  1.5 0.0 copy-start.2
  1.5 1.0 copy-done.2
  2.5 1.0 copy-done.4
  3.5 0.7 copy-done.7
  4.2 0.7 copy-done.16
  4.9 1.0 start.1
  6.0 29.6 %gather_and_send.1 = (bf16[1024,1024]{1,0:T(8,128)(2,1)S(1)}, bf16[2,256,1024]{2,1,0:T(8,128)(2,1)S(1)}) custom-call(bf16[256,1024]{1,0:T(8,128)(2,1)S(1)} %get-tuple-element.36.normed_ref, bf16[512,1024]{1,0:T(8,128)(2,1)S(1)} %get-tuple-element.37.send_ref), custom_call_target="tpu_custom_call" | custom-call | bytes 41943040 | tf_op jit(solution)/shard_map/gather_and_send/pallas_call | solution.py:268
  35.6 0.0 copy-start.12
  35.6 1.1 collective-permute-start
  36.7 1.7 collective-permute-start.1
  38.4 21.7 %collective-permute-done.g1_ref = bf16[2,256,1024]{2,1,0:T(8,128)(2,1)S(1)} collective-permute-done((bf16[2,256,1024]{2,1,0:T(8,128)(2,1)S(1)}, bf16[2,256,1024]{2,1,0:T(8,128)(2,1)S(1)}, u32[]{:S(2)}, u32[]{:S(2)}) %collective-permute-start) | collective-permute-done | bytes 1048608 | tf_op jit(solution)/shard_map/ppermute | solution.py:768
  60.1 0.1 collective-permute-start.2
  60.3 2.9 collective-permute-start.3
  63.2 18.3 %attention_forward.1 = (bf16[1024,256]{1,0:T(8,128)(2,1)S(1)}, bf16[1024,256]{1,0:T(8,128)(2,1)S(1)}, bf16[1024,256]{1,0:T(8,128)(2,1)S(1)}, bf16[1024,256]{1,0:...) custom-call(bf16[1024,1024]{1,0:T(8,128)(2,1)} %copy-done.12, bf16[3,1024,256]{2,1,0:T(8,128)(2,1)S(1)} %copy-done.14, ...), custom_call_target="tpu_custom_call" | custom-call | flops 6000000000 | bytes 8388608 | tf_op jit(solution)/shard_map/attention_forward/pallas_call | solution.py:334
  81.5 0.8 copy-done.17
  82.3 0.8 copy-done.18
  83.1 1.6 copy-done.1
  84.7 69.0 %reduce_norm_send.1 = (f32[256,1024]{1,0:T(8,128)S(1)}, bf16[2,1024,1024]{2,1,0:T(8,128)(2,1)S(1)}) custom-call(bf16[1024,1024]{1,0:T(8,128)(2,1)S(1)} %copy-done.1, bf16[256,1024]{1,0:T(8,128)(2,1)S(1)} %copy-done.3, f32[1,1024]{1,0:T(1,128)S(1)} %bitcast.58, f32[1,1024]{1,0:T(1,128)S(1)} %bitcast.62, bf16[256,512]{1,0:T(8,128)(2,1)S(1)} %get-tuple-element.40.pick_ref), custom_call_target="tpu_custom_call" | custom-call | bytes 104857600 | tf_op jit(solution)/shard_map/reduce_norm_send/pallas_call | solution.py:417
  153.7 0.0 copy-start.10
  153.7 2.0 copy-done.10
  155.7 21.0 %experts.1 = (bf16[2,1024,1024]{2,1,0:T(8,128)(2,1)}, bf16[2,1024,1024]{2,1,0:T(8,128)(2,1)}, bf16[2,1024,1024]{2,1,0:T(8,128)(2,1)}, bf16[2,1024,1024]{2,1,0:T(8,128)(2,1)}) custom-call(bf16[2,1024,1024]{2,1,0:T(8,128)(2,1)} %copy-done.10, bf16[2,256,1024]{2,1,0:T(8,128)(2,1)S(1)} %get-tuple-element.42.g0_ref, ...), custom_call_target="tpu_custom_call" | custom-call | flops 12999999488 | bytes 33554432 | tf_op jit(solution)/shard_map/experts/pallas_call | solution.py:470
  176.7 7.0 %convolution_convert_fusion = bf16[2,1024,1024]{2,1,0:T(8,128)(2,1)S(1)} fusion(bf16[2,1024,1024]{2,1,0:T(8,128)(2,1)} %get-tuple-element.53, bf16[2,1024,1024]{2,1,0:T(8,128)(2,1)S(1)} %copy-done.20), kind=kOutput, calls=%fused_computation | convolution fusion | flops 4297064448 | bytes 12582912 | tf_op jit(solution)/shard_map/lrf,lfd->lrd/dot_general | solution.py:792
  183.7 1.0 slice_bitcast_fusion.5
  184.6 1.7 collective-permute-start.6
  186.3 2.7 collective-permute-start.8
  189.0 84.1 %reduce_back_gather.1 = (f32[256,1024]{1,0:T(8,128)S(1)}, bf16[1024,1024]{1,0:T(8,128)(2,1)S(1)}, f32[8,1024]{1,0:T(8,128)S(1)}) custom-call(bf16[2,1024,1024]{2,1,0:T(8,128)(2,1)S(1)} %copy-done, bf16[256,512]{1,0:T(8,128)(2,1)S(1)} %get-tuple-element.40.pick_ref, f32[256,1024]{1,0:T(8,128)S(1)} %get-tuple-element.44.residual_ref, ...), custom_call_target="tpu_custom_call" | custom-call | bytes 104857600 | tf_op jit(solution)/shard_map/reduce_back_gather/pallas_call | solution.py:561
  273.1 1.3 copy-done.13
  274.4 22.4 %attention_backward.1 = (bf16[1024,1024]{1,0:T(8,128)(2,1)}, bf16[4096,256]{1,0:T(8,128)(2,1)}) custom-call(bf16[1024,1024]{1,0:T(8,128)(2,1)} %copy-done.13, bf16[256,1024]{1,0:T(8,128)(2,1)S(1)} %copy-done.15, bf16[3,1024,256]{2,1,0:T(8,128)(2,1)} %wqkv_ref.3, bf16[1024,1024]{1,0:T(8,128)(2,1)} %copy-done.12, ...), custom_call_target="tpu_custom_call" | custom-call | flops 12000000000 | bytes 12582912 | tf_op jit(solution)/shard_map/attention_backward/pallas_call | solution.py:625
  296.8 1.2 fusion.3
  298.1 1.0 collective-permute-start.5
  299.1 9.2 %fusion.9 = f32[2,1024,1024]{2,1,0:T(8,128)} fusion(bf16[2,1024,1024]{2,1,0:T(8,128)(2,1)S(1)} %copy-done.11, bf16[2,1024,1024]{2,1,0:T(8,128)(2,1)} %get-tuple-element.60), kind=kOutput, calls=%fused_computation.26 | convolution fusion | flops 4294967296 | bytes 16777216 | tf_op jit(solution)/shard_map/lrd,lrf->ldf/dot_general | solution.py:803
  308.2 3.3 collective-permute-done.5
  311.6 1.7 fusion.6
  313.3 0.8 collective-permute-start.9
  314.1 6.8 %fusion.10 = f32[2,1024,1024]{2,1,0:T(8,128)} fusion(bf16[2,1024,1024]{2,1,0:T(8,128)(2,1)S(1)} %copy-done.21, bf16[2,1024,1024]{2,1,0:T(8,128)(2,1)S(1)} %copy-done.22), kind=kOutput, calls=%fused_computation.27 | convolution fusion | flops 4294967296 | bytes 16777216 | tf_op jit(solution)/shard_map/lrf,lrd->lfd/dot_general | solution.py:804
  320.9 3.6 collective-permute-done.9
  324.4 1.3 fusion.7
  325.7 0.1 pad_maximum_fusion.mixed_ref
  325.9 65.9 %last_sums.1 = (bf16[256,1024]{1,0:T(8,128)(2,1)S(1)}, f32[256,1024]{1,0:T(8,128)S(1)}, bf16[4096,256]{1,0:T(8,128)(2,1)}, f32[8,1024]{1,0:T(8,128)S(1)}) custom-call(bf16[1024,1024]{1,0:T(8,128)(2,1)} %get-tuple-element.51.term_ref, f32[256,1024]{1,0:T(8,128)S(1)} %get-tuple-element.52.gres_ref, bf16[256,1024]{1,0:T(8,128)(2,1)S(1)} %copy-done.3, ...), custom_call_target="tpu_custom_call" | custom-call | bytes 104857600 | tf_op jit(solution)/shard_map/last_sums/pallas_call | solution.py:738
  391.7 1.5 slice.60
  393.2 1.1 slice.61
  394.3 0.6 fusion.8
  394.9 1.9 convert.12
  396.9 0.1 convert_bitcast_fusion
  397.0 1.1 copy.27
  398.1 0.8 copy.30
  398.9 1.0 copy.31
  (45 shorter events, 0.2 us)
Async XLA Ops:
  1.5 1.0 copy-start.2
  2.5 1.0 copy-start.4
  3.5 0.7 copy-start.7
  4.2 0.7 copy-start.16
  4.9 58.3 %copy-start.14 = (bf16[3,1024,256]{2,1,0:T(8,128)(2,1)S(1)}, bf16[3,1024,256]{2,1,0:T(8,128)(2,1)}, u32[]{:S(2)}) copy-start(bf16[3,1024,256]{2,1,0:T(8,128)(2,1)} %wqkv_ref.3) | copy-start | bytes 4718596
  4.9 58.3 %copy-start.15 = (bf16[256,1024]{1,0:T(8,128)(2,1)S(1)}, bf16[256,1024]{1,0:T(8,128)(2,1)}, u32[]{:S(2)}) copy-start(bf16[256,1024]{1,0:T(8,128)(2,1)} %wout_ref.3) | copy-start | bytes 1572868
  35.6 27.6 %copy-start.12 = (bf16[1024,1024]{1,0:T(8,128)(2,1)}, bf16[1024,1024]{1,0:T(8,128)(2,1)S(1)}, u32[]{:S(2)}) copy-start(bf16[1024,1024]{1,0:T(8,128)(2,1)S(1)} %get-tuple-element.38.joined_ref) | copy-start | bytes 6291460
  35.6 24.5 %collective-permute-start = (bf16[2,256,1024]{2,1,0:T(8,128)(2,1)S(1)}, bf16[2,256,1024]{2,1,0:T(8,128)(2,1)S(1)}, u32[]{:S(2)}, u32[]{:S(2)}) collective-permute-start(bf16[2,256,1024]{2,1,0:T(8,128)(2,1)S(1)} %get-tuple-element.42.g0_ref), channel_id=1, source_target_pairs={{0,1},{1,2},{2,3},{3,0},{4,5},{5,6},{6,7},{7,4},{8,9},{9,10},{10,1... | collective-permute-start | bytes 3145736 | tf_op jit(solution)/shard_map/ppermute | solution.py:768
  36.7 23.5 %collective-permute-start.1 = (bf16[2,256,1024]{2,1,0:T(8,128)(2,1)S(1)}, bf16[2,256,1024]{2,1,0:T(8,128)(2,1)S(1)}, u32[]{:S(2)}, u32[]{:S(2)}) collective-permute-start(bf16[2,256,1024]{2,1,0:T(8,128)(2,1)S(1)} %get-tuple-element.42.g0_ref), channel_id=1, source_target_pairs={{0,3},{1,0},{2,1},{3,2},{4,7},{5,4},{6,5},{7,6},{8,11},{9,8},{10,9... | collective-permute-start | bytes 3145736 | tf_op jit(solution)/shard_map/ppermute | solution.py:768
  60.1 95.6 %collective-permute-start.2 = (bf16[256,1024]{1,0:T(8,128)(2,1)S(1)}, bf16[256,1024]{1,0:T(8,128)(2,1)S(1)}, u32[]{:S(2)}, u32[]{:S(2)}) collective-permute-start(bf16[256,1024]{1,0:T(8,128)(2,1)S(1)} %slice_bitcast_fusion.9), channel_id=1, source_target_pairs={{0,1},{1,2},{2,3},{3,0},{4,5},{5,6},{6,7},{7,4},{8,9},{9,10},{10,1... | collective-permute-start | bytes 1572872 | tf_op jit(solution)/shard_map/ppermute | solution.py:768
  60.3 95.4 %collective-permute-start.3 = (bf16[256,1024]{1,0:T(8,128)(2,1)S(1)}, bf16[256,1024]{1,0:T(8,128)(2,1)S(1)}, u32[]{:S(2)}, u32[]{:S(2)}) collective-permute-start(bf16[256,1024]{1,0:T(8,128)(2,1)S(1)} %slice_bitcast_fusion.8), channel_id=1, source_target_pairs={{0,3},{1,0},{2,1},{3,2},{4,7},{5,4},{6,5},{7,6},{8,11},{9,8},{10,9... | collective-permute-start | bytes 1572872 | tf_op jit(solution)/shard_map/ppermute | solution.py:768
  63.2 19.9 %copy-start.3 = (bf16[256,1024]{1,0:T(8,128)(2,1)S(1)}, bf16[256,1024]{1,0:T(8,128)(2,1)}, u32[]{:S(2)}) copy-start(bf16[256,1024]{1,0:T(8,128)(2,1)} %x_ref.5) | copy-start | bytes 1572868
  63.2 19.9 %copy-start.6 = (f32[1024]{0:T(1024)S(1)}, f32[1024]{0:T(1024)}, u32[]{:S(2)}) copy-start(f32[1024]{0:T(1024)} %param.16) | copy-start | bytes 12292
  63.2 19.9 %copy-start.9 = (f32[1024]{0:T(1024)S(1)}, f32[1024]{0:T(1024)}, u32[]{:S(2)}) copy-start(f32[1024]{0:T(1024)} %param.17) | copy-start | bytes 12292
  81.5 0.8 copy-start.17
  82.3 0.8 copy-start.18
  83.1 1.6 copy-start.1
  153.7 2.0 copy-start.10
  155.7 21.0 %copy-start.20 = (bf16[2,1024,1024]{2,1,0:T(8,128)(2,1)S(1)}, bf16[2,1024,1024]{2,1,0:T(8,128)(2,1)}, u32[]{:S(2)}) copy-start(bf16[2,1024,1024]{2,1,0:T(8,128)(2,1)} %wdown_ref.1) | copy-start | bytes 12582916
  176.7 12.3 %copy-start.5 = (bf16[256,1024]{1,0:T(8,128)(2,1)S(1)}, bf16[256,1024]{1,0:T(8,128)(2,1)}, u32[]{:S(2)}) copy-start(bf16[256,1024]{1,0:T(8,128)(2,1)} %grad_ref.3) | copy-start | bytes 1572868
  183.6 89.4 %copy-start.19 = (bf16[2,1024,1024]{2,1,0:T(8,128)(2,1)}, bf16[2,1024,1024]{2,1,0:T(8,128)(2,1)S(1)}, u32[]{:S(2)}) copy-start(bf16[2,1024,1024]{2,1,0:T(8,128)(2,1)S(1)} %convolution_convert_fusion) | copy-start | bytes 12582916
  183.6 5.3 %copy-start = (bf16[2,1024,1024]{2,1,0:T(8,128)(2,1)S(1)}, bf16[2,1024,1024]{2,1,0:T(8,128)(2,1)}, u32[]{:S(2)}) copy-start(bf16[2,1024,1024]{2,1,0:T(8,128)(2,1)} %get-tuple-element.43.up_ref) | copy-start | bytes 12582916
  184.6 123.6 %collective-permute-start.6 = (bf16[256,1024]{1,0:T(8,128)(2,1)S(1)}, bf16[256,1024]{1,0:T(8,128)(2,1)S(1)}, u32[]{:S(2)}, u32[]{:S(2)}) collective-permute-start(bf16[256,1024]{1,0:T(8,128)(2,1)S(1)} %get-tuple-element.67), channel_id=1, source_target_pairs={{0,3},{1,0},{2,1},{3,2},{4,7},{5,4},{6,5},{7,6},{8,11},{9,8},{10,9... | collective-permute-start | bytes 1572872 | tf_op jit(solution)/shard_map/ppermute | solution.py:768
  186.3 110.5 %collective-permute-start.4 = (bf16[256,1024]{1,0:T(8,128)(2,1)}, bf16[256,1024]{1,0:T(8,128)(2,1)S(1)}, u32[]{:S(2)}, u32[]{:S(2)}) collective-permute-start(bf16[256,1024]{1,0:T(8,128)(2,1)} %get-tuple-element.64), channel_id=1, source_target_pairs={{0,1},{1,2},{2,3},{3,0},{4,5},{5,6},{6,7},{7,4},{8,9},{9,10},{10,1... | collective-permute-start | bytes 1572872 | tf_op jit(solution)/shard_map/ppermute | solution.py:768
  186.3 121.9 %collective-permute-start.8 = (bf16[256,1024]{1,0:T(8,128)(2,1)S(1)}, bf16[256,1024]{1,0:T(8,128)(2,1)S(1)}, u32[]{:S(2)}, u32[]{:S(2)}) collective-permute-start(bf16[256,1024]{1,0:T(8,128)(2,1)S(1)} %get-tuple-element.65), channel_id=1, source_target_pairs={{0,3},{1,0},{2,1},{3,2},{4,7},{5,4},{6,5},{7,6},{8,11},{9,8},{10,9... | collective-permute-start | bytes 1572872 | tf_op jit(solution)/shard_map/ppermute | solution.py:768
  189.0 131.9 %collective-permute-start.7 = (bf16[256,1024]{1,0:T(8,128)(2,1)S(1)}, bf16[256,1024]{1,0:T(8,128)(2,1)S(1)}, u32[]{:S(2)}, u32[]{:S(2)}) collective-permute-start(bf16[256,1024]{1,0:T(8,128)(2,1)S(1)} %get-tuple-element.66), channel_id=1, source_target_pairs={{0,1},{1,2},{2,3},{3,0},{4,5},{5,6},{6,7},{7,4},{8,9},{9,10},{10,1... | collective-permute-start | bytes 1572872 | tf_op jit(solution)/shard_map/ppermute | solution.py:768
  273.1 1.3 copy-start.13
  274.4 24.6 %copy-start.11 = (bf16[2,1024,1024]{2,1,0:T(8,128)(2,1)S(1)}, bf16[2,1024,1024]{2,1,0:T(8,128)(2,1)}, u32[]{:S(2)}) copy-start(bf16[2,1024,1024]{2,1,0:T(8,128)(2,1)} %copy-done.10) | copy-start | bytes 12582916
  298.1 13.5 %collective-permute-start.5 = (bf16[256,1024]{1,0:T(8,128)(2,1)S(1)}, bf16[256,1024]{1,0:T(8,128)(2,1)S(1)}, u32[]{:S(2)}, u32[]{:S(2)}) collective-permute-start(bf16[256,1024]{1,0:T(8,128)(2,1)S(1)} %fusion.3), channel_id=1, source_target_pairs={{0,1},{1,2},{2,3},{3,0},{4,5},{5,6},{6,7},{7,4},{8,9},{9,10},{10,1... | collective-permute-start | bytes 1572872 | tf_op jit(solution)/shard_map/ppermute | solution.py:768
  299.1 15.0 %copy-start.21 = (bf16[2,1024,1024]{2,1,0:T(8,128)(2,1)S(1)}, bf16[2,1024,1024]{2,1,0:T(8,128)(2,1)}, u32[]{:S(2)}) copy-start(bf16[2,1024,1024]{2,1,0:T(8,128)(2,1)} %get-tuple-element.53) | copy-start | bytes 12582916
  299.1 15.0 %copy-start.22 = (bf16[2,1024,1024]{2,1,0:T(8,128)(2,1)S(1)}, bf16[2,1024,1024]{2,1,0:T(8,128)(2,1)}, u32[]{:S(2)}) copy-start(bf16[2,1024,1024]{2,1,0:T(8,128)(2,1)} %get-tuple-element.61) | copy-start | bytes 12582916
  313.3 11.1 %collective-permute-start.9 = (bf16[256,1024]{1,0:T(8,128)(2,1)S(1)}, bf16[256,1024]{1,0:T(8,128)(2,1)S(1)}, u32[]{:S(2)}, u32[]{:S(2)}) collective-permute-start(bf16[256,1024]{1,0:T(8,128)(2,1)S(1)} %get-tuple-element.63), channel_id=1, source_target_pairs={{0,3},{1,0},{2,1},{3,2},{4,7},{5,4},{6,5},{7,6},{8,11},{9,8},{10,9... | collective-permute-start | bytes 1572872 | tf_op jit(solution)/shard_map/ppermute | solution.py:768
  320.8 5.0 %copy-start.8 = (f32[1024]{0:T(1024)S(1)}, f32[1024]{0:T(1024)}, u32[]{:S(2)}) copy-start(f32[1024]{0:T(1024)} %param.12) | copy-start | bytes 12292
